TPU v7x, 32 devices: a whole 2x2x4 slice. The times are simulated.
32 devices in a mesh: ctx: 8 (over z, y), tp: 4 (over x, core).
Axes of the slice: x: 2, y: 2, z: 4, core: 2. Of those that a mesh axis runs over, the one named last changes fastest.
Arguments:
- queries: bfloat16 [1152, 3072], P('ctx', 'tp'), may hold values from -8 to 8
- keys: bfloat16 [1152, 3072], P('ctx', 'tp'), may hold values from -8 to 8
- values: bfloat16 [1152, 3072], P('ctx', 'tp'), may hold values from -6 to 6
- positions: int32 [1152], P('ctx'), may hold values from 0 to 1151, as said below
- lambda_vecs: float32 [4, 12, 128], P(None, 'tp'), may hold values from -0.6 to 0.6
- head_gain: float32 [3072], P('tp'), may hold values from 0.5 to 1.5
- out_weight: bfloat16 [3072, 5120], P('tp'), may hold values from -0.109375 to 0.109375
- residual: bfloat16 [1152, 5120], P('ctx', 'tp'), may hold values from -3 to 3
Outputs:
- mixed: bfloat16 [1152, 5120], P('ctx', 'tp')
Inputs may be any that keep to these rules, and one draw needn't show every extreme that they name: Each aligned run of 72 rows holds 72 consecutive positions in increasing order; the runs' first positions are the multiples of 72, each once.
All inputs are finite; a program needn't handle non-finite values.
Results may differ from a plain program's by a relative error of at most 0.012.
Values may be sent and summed in bfloat16 or wider, within the bound.
A program may use at most 192 MiB of HBM per device.

v0:
```python
import math

import jax
import jax.numpy as jnp
from jax import lax
from jax.sharding import PartitionSpec as P

lambda_init = 0.2
out_factor = 0.8
norm_eps = 1e-05


def per_device(queries, keys, values, positions, lambda_vecs, head_gain, out_weight, residual):
    row_count = queries.shape[0]
    head_count = lambda_vecs.shape[1]
    head_depth = lambda_vecs.shape[2]
    score_scale = 1.0 / math.sqrt(head_depth)
    query_heads = queries.reshape(row_count, head_count, 2, head_depth)
    all_positions = lax.all_gather(positions, "ctx", axis=0, tiled=True)
    key_piece = lax.all_gather(keys, "ctx", axis=0, tiled=True)
    value_piece = lax.all_gather(values, "ctx", axis=0, tiled=True)
    piece_rows = key_piece.shape[0]
    allowed = all_positions[None, :] <= positions[:, None]
    highest = jnp.full((2, head_count, row_count), -1e30, jnp.float32)
    scores = (
        jnp.einsum(
            "ihad,jhad->ahij",
            query_heads,
            key_piece.reshape(piece_rows, head_count, 2, head_depth),
            preferred_element_type=jnp.float32,
        )
        * score_scale
    )
    scores = jnp.where(allowed, scores, -jnp.inf)
    fresh = jnp.maximum(highest, jnp.max(scores, -1))
    expo = jnp.where(allowed, jnp.exp(scores - fresh[..., None]), 0.0)
    total = jnp.sum(expo, -1)
    numerator = jnp.einsum(
        "ahij,jhe->ahie",
        expo.astype(jnp.bfloat16),
        value_piece.reshape(piece_rows, head_count, 2 * head_depth),
        preferred_element_type=jnp.float32,
    )
    highest, total, numerator = (fresh, total, numerator)
    attn = numerator / total[..., None]
    lambda_head = (
        jnp.exp(jnp.sum(lambda_vecs[0] * lambda_vecs[1], -1))
        - jnp.exp(jnp.sum(lambda_vecs[2] * lambda_vecs[3], -1))
        + lambda_init
    )
    diff = attn[0] - lambda_head[:, None, None] * attn[1]
    mean_square = jnp.mean(diff * diff, -1, keepdims=True)
    normed = (
        out_factor
        * diff
        / jnp.sqrt(mean_square + norm_eps)
        * head_gain.reshape(head_count, 1, 2 * head_depth)
    )
    normed = (
        jnp.transpose(normed, (1, 0, 2))
        .reshape(row_count, head_count * 2 * head_depth)
        .astype(jnp.bfloat16)
    )
    shares = lax.psum_scatter(
        lax.dot_general(
            out_weight, normed, (((0,), (1,)), ((), ())), preferred_element_type=jnp.float32
        ).astype(jnp.bfloat16),
        "tp",
        scatter_dimension=0,
        tiled=True,
    ).astype(jnp.float32)
    projected = jnp.transpose(shares)
    return (projected + residual.astype(jnp.float32)).astype(jnp.bfloat16)


def solution(mesh):
    placed = (
        P("ctx", "tp"),
        P("ctx", "tp"),
        P("ctx", "tp"),
        P("ctx"),
        P(None, "tp", None),
        P("tp"),
        P("tp", None),
        P("ctx", "tp"),
    )
    return jax.shard_map(
        per_device, mesh=mesh, in_specs=placed, out_specs=P("ctx", "tp"), check_vma=False
    )
```

profile of v0, /device:TPU:0, one launch (start us, length us, event | category | flops | bytes accessed | tf_op | source)
XLA Modules:
  0.0 152.9 jit_solution(16581531371516200551)
XLA Ops:
  6.5 0.0 all-gather.3.cloned.1.call-start
  6.5 0.7 all-gather.3.cloned.1.call-update
  7.3 0.0 all-gather.5.cloned.1.call-start
  7.3 0.7 all-gather.5.cloned.1.call-update
  8.0 0.0 reduce-scatter.2.cloned.1.call-start
  8.1 1.0 reshape.37
  9.1 0.7 mul.50
  9.8 1.2 dynamic-slice
  11.7 0.9 dynamic-update-slice
  12.5 13.2 %all-reduce = s32[1152]{0:T(1024)S(1)} all-reduce(s32[1152]{0:T(1024)S(1)} %dynamic-update-slice), channel_id=1, replica_groups=mesh['ctx'=8,'tp'=4] {'ctx'}, use_global_device_ids=true, to_apply=%add | all-reduce | flops 1152 | bytes 9216
  25.8 0.9 multiply_reduce_fusion.2
  26.7 0.8 broadcast_compare_fusion
  27.6 30.7 %all-gather.3.cloned.1.call-done = bf16[1152,768]{1,0:T(8,128)(2,1)} async-done(((bf16[144,768]{1,0:T(8,128)(2,1)}), bf16[1152,768]{1,0:T(8,128)(2,1)}) %all-gather.3.cloned.1.call-update) | async-done | bytes 1769488 | tf_op jit(solution)/shard_map/all_gather | solution.py:20
  58.3 2.7 %copy.20 = bf16[1152,768]{0,1:T(8,128)(2,1)S(1)} copy(bf16[1152,768]{1,0:T(8,128)(2,1)} %all-gather.3.cloned.1.call-done) | data formatting | bytes 3538944 | tf_op jit(solution)/shard_map/all_gather | solution.py:20
  61.0 1.0 fusion.18
  62.0 1.1 fusion.2
  63.1 42.4 %all-gather.5.cloned.1.call-done = bf16[1152,768]{1,0:T(8,128)(2,1)} async-done(((bf16[144,768]{1,0:T(8,128)(2,1)}), bf16[1152,768]{1,0:T(8,128)(2,1)}) %all-gather.5.cloned.1.call-update) | async-done | bytes 1769488 | tf_op jit(solution)/shard_map/all_gather | solution.py:21
  105.5 3.9 %copy.23 = bf16[1152,768]{0,1:T(8,128)(2,1)} copy(bf16[1152,768]{1,0:T(8,128)(2,1)} %all-gather.5.cloned.1.call-done) | data formatting | bytes 3538944 | tf_op jit(solution)/shard_map/all_gather | solution.py:21
  109.3 2.3 %fusion.10 = f32[2,3,144,256]{3,2,0,1:T(8,128)S(1)} fusion(bf16[1152,3,256,1]{0,2,3,1:T(8,128)(2,1)} %bitcast.45, bf16[2,3,144,1152]{3,2,1,0:T(8,128)(2,1)S(1)} %get-tuple-element.8, f32[2,3,144]{2,0,1:T(2,128)S(1)} %copy.26), kind=kOutput, calls=%fused_computation.11 | convolution fusion | flops 509829120 | bytes 4648320 | tf_op jit(solution)/shard_map/ahij,jhe->ahie/dot_general | solution.py:38
  111.6 0.3 multiply_reduce_fusion
  111.8 0.2 fusion.17
  112.0 0.0 copy-start
  112.1 5.8 %fusion = bf16[5120,144]{0,1:T(8,128)(2,1)} fusion(bf16[144,768]{1,0:T(8,128)(2,1)S(1)} %bitcast.46, bf16[768,5120]{1,0:T(8,128)(2,1)} %param.14), kind=kOutput, calls=%fused_computation.1 | convolution fusion | flops 1133199360 | bytes 9560064 | tf_op jit(solution)/shard_map/dot_general | solution.py:65
  117.8 0.0 reduce-scatter.2.cloned.1.call-update
  117.9 26.7 %reduce-scatter.2.cloned.1.call-done = bf16[1280,144]{0,1:T(8,128)(2,1)} async-done(((bf16[5120,144]{0,1:T(8,128)(2,1)}), bf16[1280,144]{0,1:T(8,128)(2,1)}) %reduce-scatter.2.cloned.1.call-update) | async-done | bytes 368656 | tf_op jit(solution)/shard_map/reduce_scatter | solution.py:64
  144.5 0.0 copy-done
  144.5 1.8 %fusion.13 = bf16[144,1280]{1,0:T(8,128)(2,1)} fusion(bf16[1280,144]{0,1:T(8,128)(2,1)} %reduce-scatter.2.cloned.1.call-done, bf16[144,1280]{1,0:T(8,128)(2,1)S(1)} %copy-done), kind=kLoop, calls=%fused_computation.13 | loop fusion | flops 737280 | bytes 1105920 | tf_op jit(solution)/shard_map/convert_element_type | solution.py:73
  (6 shorter events, 0.1 us)
Async XLA Ops:
  6.5 51.8 %all-gather.3.cloned.1.call-start = ((), (), s32[]{:S(2)}) async-start(), calls=%async_computation.1 | async-start | bytes 1990656 | tf_op jit(solution)/shard_map/all_gather | solution.py:20
  7.3 98.2 %all-gather.5.cloned.1.call-start = ((), (), s32[]{:S(2)}) async-start(), calls=%async_computation.2 | async-start | bytes 1990656 | tf_op jit(solution)/shard_map/all_gather | solution.py:21
  8.0 136.5 %reduce-scatter.2.cloned.1.call-start = ((), (), s32[]{:S(2)}) async-start(), calls=%async_computation.3 | async-start | bytes 1843200 | tf_op jit(solution)/shard_map/reduce_scatter | solution.py:64
  112.0 32.5 %copy-start = (bf16[144,1280]{1,0:T(8,128)(2,1)S(1)}, bf16[144,1280]{1,0:T(8,128)(2,1)}, u32[]{:S(2)}) copy-start(bf16[144,1280]{1,0:T(8,128)(2,1)} %param.15) | copy-start | bytes 1105924
Sparse Core Ops, SparseCore 0:
  9.5 48.7 all-gather.2
  60.5 44.9 all-gather.4
  118.0 26.5 reduce-scatter.1
where the time goes:
time: 153 us
  waiting for transfers between devices  101 us (66%)
  between operations  13.8 us (9%)
  blocking collectives  13.2 us (9%)
  local copies, waits for them, and re-layouts  10.4 us (7%)
  matrix products  9.01 us (6%)
  other arithmetic  5.13 us (3%)
    all_gather x1, waiting for transfers between devices, per_device(): value_piece = lax.all_gather(values, 'ctx', axis=0, tiled=True)  42.4 us
    all_gather x1, waiting for transfers between devices, per_device(): key_piece = lax.all_gather(keys, 'ctx', axis=0, tiled=True)  30.7 us
    reduce_scatter x1, waiting for transfers between devices, per_device(): lax.psum_scatter(lax.dot_general(out_weight, normed, (((0,), (1,)), ((),...  26.7 us
    unnamed x1, blocking collectives  13.2 us
    dot_general x1, matrix products, per_device(): lax.dot_general(out_weight, normed, (((0,), (1,)), ((), ())), preferred_e...  5.78 us
    all_gather x1, local copies, waits for them, and re-layouts, per_device(): value_piece = lax.all_gather(values, 'ctx', axis=0, tiled=True)  3.85 us
  transfers between devices with their start and end apart: 3, of which 3 were waited for; matrix products, arithmetic and copies ran while one was open for 7% of the time, Pallas kernels for 0%

commit v1 on v0

v1 whole, which is shorter than its diff:
```python
import functools
import math

import jax
import jax.numpy as jnp
from jax import lax
from jax.experimental import pallas as pl
from jax.experimental.pallas import tpu as pltpu
from jax.sharding import PartitionSpec as P

lambda_init = 0.2
out_factor = 0.8
norm_eps = 1e-05
MASKED = -3e38
LOWEST = -1e30
CHUNK = 256


def layer_kernel(
    n_ctx,
    n_tp,
    q_in,
    k_in,
    v_in,
    pos_in,
    lam_in,
    gain_in,
    w_in,
    out_ref,
    q_buf,
    kv_buf,
    pos_all,
    lam_buf,
    gain_buf,
    lam_wide,
    gain_wide,
    high,
    total,
    acc,
    stage,
    normed,
    w_buf,
    part,
    got,
    init_send,
    init_recv,
    small_send,
    small_recv,
    pos_send,
    pos_recv,
    line_send,
    line_recv,
    sib_send,
    sib_recv,
    o_send,
    o_recv,
    w_local,
    w_send,
    w_recv,
    p_send,
    p_recv,
):
    heads, rows, wide = q_buf.shape
    depth = wide // 2
    W = n_ctx // 2
    X = n_tp // 2
    n_chunk = w_buf.shape[1]
    scale = 1.0 / math.sqrt(depth)
    ctx = lax.axis_index("ctx")
    tp = lax.axis_index("tp")
    w, y = lax.div(ctx, 2), lax.rem(ctx, 2)
    x, c = lax.div(tp, 2), lax.rem(tp, 2)
    crossed = c != y
    straight = c == y

    def dev(a, b):
        return {"ctx": a, "tp": b}

    def remote(src, dst, send, recv, to):
        return pltpu.make_async_remote_copy(
            src_ref=src, dst_ref=dst, send_sem=send, recv_sem=recv, device_id=to, device_id_type=pl.DeviceIdType.MESH
        )

    partner = dev(2 * w + c, 2 * x + y)
    sibling = dev(ctx, 2 * x + 1 - c)

    barrier = pltpu.get_barrier_semaphore()

    def greet(to):
        pl.semaphore_signal(barrier, inc=1, device_id=to, device_id_type=pl.DeviceIdType.MESH)

    greet(sibling)

    @pl.when(crossed)
    def _():
        greet(partner)

    for i in range(1, X):
        greet(dev(ctx, 2 * lax.rem(x + i, X) + c))

    def greet_row(i, _):
        greet(dev(lax.rem(ctx + i, n_ctx), tp))
        return 0

    lax.fori_loop(1, n_ctx, greet_row, 0)
    pl.semaphore_wait(barrier, n_ctx - 1 + 1 + X - 1 + lax.rem(c + y, 2))

    def init_pairs(h):
        cols = pl.ds(h * wide, wide)
        return (
            (k_in.at[:, cols], kv_buf.at[h, w, y, :, pl.ds(0, wide)]),
            (v_in.at[:, cols], kv_buf.at[h, w, y, :, pl.ds(wide, wide)]),
            (q_in.at[:, cols], q_buf.at[h]),
        )

    small_pairs = ((lam_in, lam_buf), (gain_in, gain_buf))

    @pl.when(straight)
    def _():
        for h in range(heads):
            for j, (src, dst) in enumerate(init_pairs(h)):
                pltpu.make_async_copy(src, dst, init_recv.at[h, j]).start()
        for j, (src, dst) in enumerate(small_pairs):
            pltpu.make_async_copy(src, dst, small_recv.at[j]).start()

    @pl.when(crossed)
    def _():
        for h in range(heads):
            for j, (src, dst) in enumerate(init_pairs(h)):
                remote(src, dst, init_send.at[h, j], init_recv.at[h, j], partner).start()
        for j, (src, dst) in enumerate(small_pairs):
            remote(src, dst, small_send.at[j], small_recv.at[j], partner).start()

    def pos_copy(i):
        return remote(
            pos_in,
            pos_all.at[ctx],
            pos_send.at[i],
            pos_recv.at[ctx],
            dev(lax.rem(ctx + i, n_ctx), tp),
        )

    def pos_start(i, _):
        pos_copy(i).start()
        return 0

    lax.fori_loop(1, n_ctx, pos_start, 0)
    pos_all[ctx] = pos_in[...]

    col_count = n_chunk * CHUNK
    w_rows = heads * wide

    def w_src(i, j, core):
        start = pl.multiple_of((2 * i + core) * col_count + j * CHUNK, CHUNK)
        return w_in.at[:, pl.ds(start, CHUNK)]

    def w_dst(i, j):
        return w_buf.at[i, j, pl.ds(pl.multiple_of(c * w_rows, 16), w_rows)]

    def w_own(i, j):
        return pltpu.make_async_copy(w_src(i, j, c), w_dst(i, j), w_local.at[i, j])

    def w_give(i, j):
        return remote(w_src(i, j, 1 - c), w_dst(i, j), w_send.at[i, j], w_recv.at[i, j], sibling)

    def w_take(i, j):
        dst = w_buf.at[i, j, pl.ds(pl.multiple_of((1 - c) * w_rows, 16), w_rows)]
        return remote(w_src(i, j, c), dst, w_send.at[i, j], w_recv.at[i, j], sibling)

    def line_copy(h, idx, way):
        block = kv_buf.at[h, idx, c]
        to = dev(ctx + (2 if way else -2), tp)
        return remote(block, block, line_send.at[way, h, idx], line_recv.at[h, idx], to)

    def sib_copy(h, idx):
        block = kv_buf.at[h, idx, c]
        return remote(block, block, sib_send.at[h, idx], sib_recv.at[h, idx], sibling)

    def sib_wait(h, idx):
        block = kv_buf.at[h, idx, 1 - c]
        remote(block, block, sib_send.at[h, idx], sib_recv.at[h, idx], sibling).wait_recv()

    def attend(h, idx):
        q_pos = high_q()
        k_pos = jnp.concatenate([pos_all[2 * idx], pos_all[2 * idx + 1]], axis=1)
        allowed = k_pos <= q_pos
        value = kv_buf[h, idx, :, :, pl.ds(wide, wide)].reshape(2 * rows, wide)
        for a in range(2):
            query = q_buf[h, :, pl.ds(a * depth, depth)]
            key = kv_buf[h, idx, :, :, pl.ds(a * depth, depth)].reshape(2 * rows, depth)
            scores = (
                lax.dot_general(query, key, (((1,), (1,)), ((), ())), preferred_element_type=jnp.float32) * scale
            )
            scores = jnp.where(allowed, scores, MASKED)
            before = high[h, a]
            now = jnp.maximum(before, jnp.max(scores, -1, keepdims=True))
            keep = jnp.exp(before - now)
            expo = jnp.exp(scores - now)
            high[h, a] = now
            total[h, a] = total[h, a] * keep + jnp.sum(expo, -1, keepdims=True)
            acc[h, a] = acc[h, a] * keep + jnp.dot(
                expo.astype(jnp.bfloat16), value, preferred_element_type=jnp.float32
            )

    def high_q():
        line = pos_all[2 * w + c]
        square = (rows, rows)
        same = lax.broadcasted_iota(jnp.int32, square, 0) == lax.broadcasted_iota(jnp.int32, square, 1)
        return jnp.sum(jnp.where(same, jnp.broadcast_to(line, square), 0), -1, keepdims=True)

    def o_copy(h, core):
        cols = pl.ds(pl.multiple_of((y * heads + h) * wide, wide), wide)
        return remote(
            stage.at[h], normed.at[:, cols], o_send.at[core, h], o_recv.at[y, h], dev(2 * w + c, 2 * x + core)
        )

    def o_wait(g, h):
        cols = pl.ds(pl.multiple_of((g * heads + h) * wide, wide), wide)
        remote(stage.at[h], normed.at[:, cols], o_send.at[0, h], o_recv.at[g, h], sibling).wait_recv()

    def finish(h):
        first = acc[h, 0] / total[h, 0]
        second = acc[h, 1] / total[h, 1]
        diff = first - lam_wide[h] * second
        mean_square = jnp.mean(diff * diff, -1, keepdims=True)
        result = (out_factor * diff * lax.rsqrt(mean_square + norm_eps) * gain_wide[h]).astype(jnp.bfloat16)
        stage[h] = result

        @pl.when(straight)
        def _():
            normed[:, pl.ds(pl.multiple_of((y * heads + h) * wide, wide), wide)] = result
            o_copy(h, 1 - c).start()

        @pl.when(crossed)
        def _():
            o_copy(h, 0).start()
            o_copy(h, 1).start()

    high[...] = jnp.full(high.shape, LOWEST, jnp.float32)
    total[...] = jnp.zeros(total.shape, jnp.float32)
    acc[...] = jnp.zeros(acc.shape, jnp.float32)

    def step(t, _):
        s, h = lax.div(t, heads), lax.rem(t, heads)

        @pl.when(s == 0)
        def _():
            cols = pl.ds(0, wide)
            src = k_in.at[:, cols]
            pltpu.make_async_copy(src, kv_buf.at[h, w, c, :, cols], init_recv.at[h, 0]).wait()
            pltpu.make_async_copy(src, kv_buf.at[h, w, c, :, pl.ds(wide, wide)], init_recv.at[h, 1]).wait()

            @pl.when(w > 0)
            def _():
                line_copy(h, w, 0).start()

            @pl.when(w < W - 1)
            def _():
                line_copy(h, w, 1).start()

            sib_copy(h, w).start()
            pltpu.make_async_copy(src, q_buf.at[h], init_recv.at[h, 2]).wait()

        @pl.when(t == heads)
        def _():
            for i in range(X):
                for j in range(n_chunk):
                    w_own(i, j).start()
                    w_give(i, j).start()
            for j, (src, dst) in enumerate(small_pairs):
                pltpu.make_async_copy(src, dst, small_recv.at[j]).wait()
            vecs = lam_buf[...]
            lam = (
                jnp.exp(jnp.sum(vecs[0] * vecs[1], -1, keepdims=True))
                - jnp.exp(jnp.sum(vecs[2] * vecs[3], -1, keepdims=True))
                + lambda_init
            )
            for i in range(heads):
                lam_wide[i] = jnp.broadcast_to(lam[i : i + 1], (1, wide))
                gain_wide[i] = gain_buf[:, pl.ds(i * wide, wide)]

        @pl.when((s > 0) & (s < W))
        def _():
            @pl.when(w - s >= 0)
            def _():
                line_copy(h, w - s, 1).wait_recv()

                @pl.when(w < W - 1)
                def _():
                    line_copy(h, w - s, 1).start()

                sib_copy(h, w - s).start()

            @pl.when(w + s < W)
            def _():
                line_copy(h, w + s, 0).wait_recv()

                @pl.when(w > 0)
                def _():
                    line_copy(h, w + s, 0).start()

                sib_copy(h, w + s).start()

        @pl.when(t == 1)
        def _():
            def pos_wait(i, _):
                frm = lax.rem(ctx + i, n_ctx)
                remote(pos_in, pos_all.at[frm], pos_send.at[i], pos_recv.at[frm], sibling).wait_recv()
                return 0

            lax.fori_loop(1, n_ctx, pos_wait, 0)

        @pl.when(t > 0)
        def _():
            s1, h1 = lax.div(t - 1, heads), lax.rem(t - 1, heads)

            @pl.when(w - s1 >= 0)
            def _():
                sib_wait(h1, w - s1)
                attend(h1, w - s1)

            @pl.when((s1 > 0) & (w + s1 < W))
            def _():
                sib_wait(h1, w + s1)
                attend(h1, w + s1)

            @pl.when(s1 == W - 1)
            def _():
                finish(h1)

        return 0

    lax.fori_loop(0, W * heads + 1, step, 0)

    for i in range(X):
        for j in range(n_chunk):
            w_own(i, j).wait()
            w_take(i, j).wait_recv()
    for h in range(heads):
        o_wait(1 - y, h)

        @pl.when(crossed)
        def _():
            o_wait(y, h)

    def product(i, j):
        return jnp.dot(normed[...], w_buf[i, j], preferred_element_type=jnp.float32)

    def p_copy(i, j):
        other = lax.rem(x + i, X)
        return remote(
            part.at[i - 1, j], got.at[i - 1, j], p_send.at[i - 1, j], p_recv.at[i - 1, j], dev(ctx, 2 * other + c)
        )

    for i in range(1, X):

        def send_chunk(j, _):
            part[i - 1, j] = product(lax.rem(x + i, X), j).astype(jnp.bfloat16)
            p_copy(i, j).start()
            return 0

        lax.fori_loop(0, n_chunk, send_chunk, 0)

    def own_chunk(j, _):
        out_ref[:, pl.ds(pl.multiple_of(j * CHUNK, CHUNK), CHUNK)] = product(x, j)
        return 0

    lax.fori_loop(0, n_chunk, own_chunk, 0)

    for i in range(X):
        for j in range(n_chunk):
            w_give(i, j).wait_send()

    def pos_done(i, _):
        pos_copy(i).wait_send()
        return 0

    lax.fori_loop(1, n_ctx, pos_done, 0)

    @pl.when(crossed)
    def _():
        for h in range(heads):
            for j, (src, dst) in enumerate(init_pairs(h)):
                remote(src, dst, init_send.at[h, j], init_recv.at[h, j], partner).wait_send()
            o_copy(h, 0).wait_send()
            o_copy(h, 1).wait_send()
        for j, (src, dst) in enumerate(small_pairs):
            remote(src, dst, small_send.at[j], small_recv.at[j], partner).wait_send()

    @pl.when(straight)
    def _():
        for h in range(heads):
            o_copy(h, 1 - c).wait_send()

    def line_done(idx, _):
        for h in range(heads):
            sib_copy(h, idx).wait_send()

            @pl.when((idx <= w) & (w < W - 1))
            def _():
                line_copy(h, idx, 1).wait_send()

            @pl.when((idx >= w) & (w > 0))
            def _():
                line_copy(h, idx, 0).wait_send()

        return 0

    lax.fori_loop(0, W, line_done, 0)

    for i in range(1, X):

        def add_chunk(j, _):
            p_copy(i, j).wait()
            cols = pl.ds(pl.multiple_of(j * CHUNK, CHUNK), CHUNK)
            out_ref[:, cols] += got[i - 1, j].astype(jnp.float32)
            return 0

        lax.fori_loop(0, n_chunk, add_chunk, 0)


def per_device(n_ctx, n_tp, queries, keys, values, positions, lambda_vecs, head_gain, out_weight, residual):
    rows = queries.shape[0]
    heads, depth = lambda_vecs.shape[1], lambda_vecs.shape[2]
    wide = 2 * depth
    W, X = n_ctx // 2, n_tp // 2
    columns = out_weight.shape[1] // n_tp
    n_chunk = columns // CHUNK
    vmem = pl.BlockSpec(memory_space=pltpu.VMEM)
    hbm = pl.BlockSpec(memory_space=pl.ANY)
    bf16, f32 = jnp.bfloat16, jnp.float32
    dma = pltpu.SemaphoreType.DMA
    projected = pl.pallas_call(
        functools.partial(layer_kernel, n_ctx, n_tp),
        out_shape=jax.ShapeDtypeStruct((rows, columns), f32),
        in_specs=[hbm, hbm, hbm, vmem, vmem, vmem, hbm],
        out_specs=vmem,
        scratch_shapes=[
            pltpu.VMEM((heads, rows, wide), bf16),
            pltpu.VMEM((heads, W, 2, rows, 2 * wide), bf16),
            pltpu.VMEM((n_ctx, 1, rows), jnp.int32),
            pltpu.VMEM(lambda_vecs.shape, f32),
            pltpu.VMEM((1, heads * wide), f32),
            pltpu.VMEM((heads, 1, wide), f32),
            pltpu.VMEM((heads, 1, wide), f32),
            pltpu.VMEM((heads, 2, rows, 1), f32),
            pltpu.VMEM((heads, 2, rows, 1), f32),
            pltpu.VMEM((heads, 2, rows, wide), f32),
            pltpu.VMEM((heads, rows, wide), bf16),
            pltpu.VMEM((rows, 2 * heads * wide), bf16),
            pltpu.VMEM((X, n_chunk, 2 * heads * wide, CHUNK), bf16),
            pltpu.VMEM((X - 1, n_chunk, rows, CHUNK), bf16),
            pltpu.VMEM((X - 1, n_chunk, rows, CHUNK), bf16),
            dma((heads, 3)),
            dma((heads, 3)),
            dma((2,)),
            dma((2,)),
            dma((n_ctx,)),
            dma((n_ctx,)),
            dma((2, heads, W)),
            dma((heads, W)),
            dma((heads, W)),
            dma((heads, W)),
            dma((2, heads)),
            dma((2, heads)),
            dma((X, n_chunk)),
            dma((X, n_chunk)),
            dma((X, n_chunk)),
            dma((X - 1, n_chunk)),
            dma((X - 1, n_chunk)),
        ],
        compiler_params=pltpu.CompilerParams(
            collective_id=0, has_side_effects=True, vmem_limit_bytes=56 * 1024 * 1024
        ),
        name="attend_and_project",
    )(
        queries,
        keys,
        values,
        positions.reshape(1, rows),
        lambda_vecs,
        head_gain.reshape(1, heads * wide),
        out_weight,
    )
    return (projected + residual.astype(f32)).astype(bf16)


def solution(mesh):
    placed = (
        P("ctx", "tp"),
        P("ctx", "tp"),
        P("ctx", "tp"),
        P("ctx"),
        P(None, "tp", None),
        P("tp"),
        P("tp", None),
        P("ctx", "tp"),
    )
    return jax.shard_map(
        functools.partial(per_device, mesh.shape["ctx"], mesh.shape["tp"]),
        mesh=mesh,
        in_specs=placed,
        out_specs=P("ctx", "tp"),
        check_vma=False,
    )
```

time: 153 us -> 62.1 us (0.41)
  waiting for transfers between devices: 101 us -> 0 us
  Pallas kernels: 0 us -> 57.2 us
  between operations: 13.8 us -> 0.02 us
  blocking collectives: 13.2 us -> 0 us
  matrix products: 9.01 us -> 0 us
  local copies, waits for them, and re-layouts: 10.4 us -> 2.61 us
  other arithmetic: 5.13 us -> 1.92 us
    all_gather x2 -> x0, waiting for transfers between devices: 73.1 us -> none  [the longest x1 42.4 us: per_device(): value_piece = lax.all_gather(values, 'ctx', axis=0, tiled=True)]
    pallas_call x0 -> x1, Pallas kernels: none -> 57.2 us  [per_device(): pl.pallas_call(functools.partial(layer_kernel, n_ctx, n_tp), out_shape=ja...]
    reduce_scatter x1 -> x0, waiting for transfers between devices: 26.7 us -> none  [per_device(): lax.psum_scatter(lax.dot_general(out_weight, normed, (((0,), (1,)), ((),...]
    unnamed x1 -> x0, blocking collectives: 13.2 us -> none
    dot_general x3 -> x0, matrix products: 9.01 us -> none  [the longest x1 5.78 us: per_device(): lax.dot_general(out_weight, normed, (((0,), (1,)), ((), ())), preferred_e...]
    all_gather x2 -> x0, local copies, waits for them, and re-layouts: 6.58 us -> none  [the longest x1 3.85 us: per_device(): value_piece = lax.all_gather(values, 'ctx', axis=0, tiled=True)]
    reduce_sum x3 -> x0, other arithmetic: 2.28 us -> none  [the longest x1 1.09 us: per_device(): total = jnp.sum(expo, -1)]
  transfers between devices with their start and end apart: 3 -> 0, of which waited for: 3 -> 0; matrix products, arithmetic and copies ran while one was open for 7% -> 0% of each run, Pallas kernels for 0% -> 0%
where the time goes in v1:
time: 62.1 us; the launch traced here: 61.8 us
  Pallas kernels  57.2 us (92%)
  local copies, waits for them, and re-layouts  2.61 us (4%)
  other arithmetic  1.92 us (3%)
    pallas_call x1, Pallas kernels, per_device(): pl.pallas_call(functools.partial(layer_kernel, n_ctx, n_tp), out_shape=ja...  57.2 us
    convert_element_type x1, other arithmetic, per_device(): return (projected + residual.astype(f32)).astype(bf16)  1.92 us
    reshape x1, local copies, waits for them, and re-layouts, per_device(): head_gain.reshape(1, heads * wide)  1.31 us
    unnamed x3, local copies, waits for them, and re-layouts  1.29 us

profile of v1, /device:TPU:0, one launch (start us, length us, event | category | flops | bytes accessed | tf_op | source)
XLA Modules:
  0.0 61.8 jit_solution(14159830259448547189)
XLA Ops:
  0.0 0.0 copy-start
  0.0 1.3 %reshape.7.gain_in = f32[1,768]{1,0:T(1,128)} reshape(f32[768]{0:T(1024)} %param.13) | data formatting | bytes 6144 | tf_op jit(solution)/shard_map/reshape | solution.py:482
  1.3 1.3 %copy.9.lam_in = f32[4,3,128]{2,1,0:T(4,128)} copy(f32[4,3,128]{2,0,1:T(4,128)} %param.12) | data formatting | bytes 12288 | tf_op args[4]
  2.6 57.2 %attend_and_project.1 = f32[144,1280]{1,0:T(8,128)} custom-call(bf16[144,768]{1,0:T(8,128)(2,1)} %q_in.1, bf16[144,768]{1,0:T(8,128)(2,1)} %k_in.1, bf16[144,768]{1,0:T(8,128)(2,1)} %v_in.1, s32[1,144]{1,0:T(1,128)} %bitcast.1, f32[4,3,128]{2,1,0:T(4,128)} %copy.9.lam_in, f32[1,768]{1,0:T(1,128)} %reshape.7.gain_in, bf16[768,5120]{1,0:T(8,128)(2,1)} %w_in.1), custom_call_target="tpu_custom_call" | custom-call | tf_op jit(solution)/shard_map/attend_and_project/pallas_call | solution.py:433
  59.8 0.0 copy-done
  59.8 1.9 %add_convert_fusion = bf16[144,1280]{1,0:T(8,128)(2,1)} fusion(f32[144,1280]{1,0:T(8,128)} %attend_and_project.1, bf16[144,1280]{1,0:T(8,128)(2,1)S(1)} %copy-done), kind=kLoop, calls=%fused_computation | loop fusion | flops 552960 | bytes 1474560 | tf_op jit(solution)/shard_map/convert_element_type | solution.py:485
Async XLA Ops:
  0.0 59.8 %copy-start = (bf16[144,1280]{1,0:T(8,128)(2,1)S(1)}, bf16[144,1280]{1,0:T(8,128)(2,1)}, u32[]{:S(2)}) copy-start(bf16[144,1280]{1,0:T(8,128)(2,1)} %param.15) | copy-start | bytes 1105924

commit v2 on v1

v2 whole, which is shorter than its diff:
```python
import functools
import math

import jax
import jax.numpy as jnp
from jax import lax
from jax.experimental import pallas as pl
from jax.experimental.pallas import tpu as pltpu
from jax.sharding import PartitionSpec as P

lambda_init = 0.2
out_factor = 0.8
norm_eps = 1e-05
MASKED = -3e38
LOWEST = -1e30
CHUNK = 256


def layer_kernel(
    n_ctx,
    n_tp,
    q_in,
    k_in,
    v_in,
    pos_in,
    lam_in,
    gain_in,
    w_in,
    res_in,
    out_ref,
    q_buf,
    kv_buf,
    pos_all,
    lam_buf,
    gain_buf,
    lam_wide,
    gain_wide,
    q_pos,
    high,
    total,
    acc,
    stage,
    normed,
    w_buf,
    res_buf,
    part_sib,
    got_sib,
    part,
    got,
    init_send,
    init_recv,
    small_send,
    small_recv,
    pos_send,
    pos_recv,
    line_send,
    line_recv,
    sib_send,
    sib_recv,
    q_send,
    q_recv,
    o_send,
    o_recv,
    w_sem,
    res_sem,
    ps_send,
    ps_recv,
    p_send,
    p_recv,
):
    heads, rows, wide = stage.shape
    heads -= 1
    depth = wide // 2
    W = n_ctx // 2
    X = n_tp // 2
    n_chunk = w_buf.shape[1]
    off = heads - 1 if W >= 4 else -1
    scale = 1.0 / math.sqrt(depth)
    ctx = lax.axis_index("ctx")
    tp = lax.axis_index("tp")
    w, y = lax.div(ctx, 2), lax.rem(ctx, 2)
    x, c = lax.div(tp, 2), lax.rem(tp, 2)
    crossed = c != y
    straight = c == y
    at_end = (off >= 0) & ((w == 0) | (w == W - 1))
    helper = (off >= 0) & ((w == 1) | (w == W - 2))
    mate = jnp.where(w == 0, 1, jnp.where(w == W - 1, W - 2, jnp.where(w == 1, 0, jnp.where(w == W - 2, W - 1, w))))

    def left_out(h):
        return at_end & (h == off)

    def goes(way, h):
        if way:
            return (w < W - 1) & ((w != W - 2) | (h != off))
        return (w > 0) & ((w != 1) | (h != off))

    def slots(h):
        return 1 + jnp.where(helper & (h == off), 1, 0)

    def dev(a, b):
        return {"ctx": a, "tp": b}

    def remote(src, dst, send, recv, to):
        return pltpu.make_async_remote_copy(
            src_ref=src, dst_ref=dst, send_sem=send, recv_sem=recv, device_id=to, device_id_type=pl.DeviceIdType.MESH
        )

    partner = dev(2 * w + c, 2 * x + y)
    sibling = dev(ctx, 2 * x + 1 - c)
    far = dev(2 * mate + c, 2 * x + y)

    barrier = pltpu.get_barrier_semaphore()

    def greet(to):
        pl.semaphore_signal(barrier, inc=1, device_id=to, device_id_type=pl.DeviceIdType.MESH)

    greet(sibling)

    @pl.when(crossed)
    def _():
        greet(partner)

    @pl.when(crossed & (at_end | helper))
    def _():
        greet(far)

    for i in range(1, X):
        greet(dev(ctx, 2 * lax.rem(x + i, X) + c))

    def greet_row(i, _):
        greet(dev(lax.rem(ctx + i, n_ctx), tp))
        return 0

    lax.fori_loop(1, n_ctx, greet_row, 0)
    pl.semaphore_wait(barrier, n_ctx - 1 + 1 + X - 1 + lax.rem(c + y, 2) + jnp.where(crossed & (at_end | helper), 1, 0))

    def init_pairs(h):
        cols = pl.ds(h * wide, wide)
        return (
            (k_in.at[:, cols], kv_buf.at[h, w, y, :, pl.ds(0, wide)]),
            (v_in.at[:, cols], kv_buf.at[h, w, y, :, pl.ds(wide, wide)]),
            (q_in.at[:, cols], q_buf.at[h]),
        )

    small_pairs = ((lam_in, lam_buf), (gain_in, gain_buf))

    @pl.when(straight)
    def _():
        for h in range(heads):
            for j, (src, dst) in enumerate(init_pairs(h)):
                pltpu.make_async_copy(src, dst, init_recv.at[h, j]).start()
        for j, (src, dst) in enumerate(small_pairs):
            pltpu.make_async_copy(src, dst, small_recv.at[j]).start()

    @pl.when(crossed)
    def _():
        for h in range(heads):
            for j, (src, dst) in enumerate(init_pairs(h)):
                remote(src, dst, init_send.at[h, j], init_recv.at[h, j], partner).start()
        for j, (src, dst) in enumerate(small_pairs):
            remote(src, dst, small_send.at[j], small_recv.at[j], partner).start()

    def pos_copy(i):
        return remote(
            pos_in,
            pos_all.at[ctx],
            pos_send.at[i],
            pos_recv.at[ctx],
            dev(lax.rem(ctx + i, n_ctx), tp),
        )

    def pos_start(i, _):
        pos_copy(i).start()
        return 0

    pltpu.make_async_copy(pos_in, pos_all.at[ctx], pos_recv.at[ctx]).start()
    lax.fori_loop(1, n_ctx, pos_start, 0)

    def w_copy(i, j):
        start = pl.multiple_of((i * n_chunk + j) * CHUNK, CHUNK)
        return pltpu.make_async_copy(w_in.at[:, pl.ds(start, CHUNK)], w_buf.at[i, j], w_sem.at[i, j])

    res_copy = pltpu.make_async_copy(res_in, res_buf, res_sem)

    def line_copy(h, idx, way):
        block = kv_buf.at[h, idx, c]
        to = dev(ctx + (2 if way else -2), tp)
        return remote(block, block, line_send.at[way, h, idx], line_recv.at[h, idx], to)

    def sib_copy(h, idx):
        block = kv_buf.at[h, idx, c]
        return remote(block, block, sib_send.at[h, idx], sib_recv.at[h, idx], sibling)

    def sib_wait(h, idx):
        block = kv_buf.at[h, idx, 1 - c]
        remote(block, block, sib_send.at[h, idx], sib_recv.at[h, idx], sibling).wait_recv()

    def q_copy():
        return remote(q_buf.at[max(off, 0)], q_buf.at[heads], q_send, q_recv, dev(2 * mate + y, tp))

    def position_column(row):
        line = pos_all[row]
        square = (rows, rows)
        same = lax.broadcasted_iota(jnp.int32, square, 0) == lax.broadcasted_iota(jnp.int32, square, 1)
        return jnp.sum(jnp.where(same, jnp.broadcast_to(line, square), 0), -1, keepdims=True)

    def attend(h, idx):
        def one(k, _):
            e = h + k * (heads - h)
            k_pos = jnp.concatenate([pos_all[2 * idx], pos_all[2 * idx + 1]], axis=1)
            allowed = k_pos <= q_pos[k]
            value = kv_buf[h, idx, :, :, pl.ds(wide, wide)].reshape(2 * rows, wide)
            before = [high[e, a] for a in range(2)]
            sums = [total[e, a] for a in range(2)]
            held = [acc[e, a] for a in range(2)]
            for a in range(2):
                query = q_buf[e, :, pl.ds(a * depth, depth)]
                key = kv_buf[h, idx, :, :, pl.ds(a * depth, depth)].reshape(2 * rows, depth)
                scores = (
                    lax.dot_general(query, key, (((1,), (1,)), ((), ())), preferred_element_type=jnp.float32) * scale
                )
                scores = jnp.where(allowed, scores, MASKED)
                now = jnp.maximum(before[a], jnp.max(scores, -1, keepdims=True))
                keep = jnp.exp(before[a] - now)
                expo = jnp.exp(scores - now)
                before[a] = now
                sums[a] = sums[a] * keep + jnp.sum(expo, -1, keepdims=True)
                held[a] = held[a] * keep + jnp.dot(
                    expo.astype(jnp.bfloat16), value, preferred_element_type=jnp.float32
                )
            for a in range(2):
                high[e, a] = before[a]
                total[e, a] = sums[a]
                acc[e, a] = held[a]
            return 0

        lax.fori_loop(0, slots(h), one, 0)

    def head_columns(h):
        return pl.ds(pl.multiple_of(h * wide, wide), wide)

    def o_copy(h, k):
        e = h + k * (heads - h)
        to = dev(2 * (w + k * (mate - w)) + c, 2 * x + y)
        return remote(stage.at[e], normed.at[:, head_columns(h)], o_send.at[e], o_recv.at[h], to)

    def finish(h):
        def one(k, _):
            e = h + k * (heads - h)
            first = acc[e, 0] / total[e, 0]
            second = acc[e, 1] / total[e, 1]
            diff = first - lam_wide[h] * second
            mean_square = jnp.mean(diff * diff, -1, keepdims=True)
            result = (out_factor * diff * lax.rsqrt(mean_square + norm_eps) * gain_wide[h]).astype(jnp.bfloat16)

            @pl.when(straight & (k == 0))
            def _():
                normed[:, head_columns(h)] = result

            @pl.when(crossed | (k > 0))
            def _():
                stage[e] = result
                o_copy(h, k).start()

            return 0

        lax.fori_loop(0, slots(h), one, 0)

    for i in range(1, n_tp + 1):
        for j in range(n_chunk):
            w_copy(lax.rem(tp + i, n_tp), j).start()
    res_copy.start()

    high[...] = jnp.full(high.shape, LOWEST, jnp.float32)
    total[...] = jnp.zeros(total.shape, jnp.float32)
    acc[...] = jnp.zeros(acc.shape, jnp.float32)

    def step(t, _):
        s, h = lax.div(t, heads), lax.rem(t, heads)

        @pl.when(s == 0)
        def _():
            cols = pl.ds(0, wide)
            src = k_in.at[:, cols]
            pltpu.make_async_copy(src, kv_buf.at[h, w, c, :, cols], init_recv.at[h, 0]).wait()
            pltpu.make_async_copy(src, kv_buf.at[h, w, c, :, pl.ds(wide, wide)], init_recv.at[h, 1]).wait()

            for way in range(2):

                @pl.when(goes(way, h))
                def _():
                    line_copy(h, w, way).start()

            @pl.when(jnp.logical_not(left_out(h)))
            def _():
                sib_copy(h, w).start()

            pltpu.make_async_copy(src, q_buf.at[h], init_recv.at[h, 2]).wait()

            @pl.when(left_out(h))
            def _():
                q_copy().start()

        @pl.when(t == heads)
        def _():
            for j, (src, dst) in enumerate(small_pairs):
                pltpu.make_async_copy(src, dst, small_recv.at[j]).wait()
            vecs = lam_buf[...]
            lam = (
                jnp.exp(jnp.sum(vecs[:, 0] * vecs[:, 1], -1, keepdims=True))
                - jnp.exp(jnp.sum(vecs[:, 2] * vecs[:, 3], -1, keepdims=True))
                + lambda_init
            )
            for i in range(heads):
                lam_wide[i] = jnp.broadcast_to(lam[i : i + 1], (1, wide))
                gain_wide[i] = jnp.concatenate([gain_buf[pl.ds(2 * i, 1)], gain_buf[pl.ds(2 * i + 1, 1)]], axis=1)

        @pl.when((s > 0) & (s < W) & jnp.logical_not(left_out(h)))
        def _():
            for way, idx in ((1, w - s), (0, w + s)):

                @pl.when((idx >= 0) & (idx < W))
                def _():
                    line_copy(h, idx, way).wait_recv()

                    @pl.when(goes(way, h))
                    def _():
                        line_copy(h, idx, way).start()

                    sib_copy(h, idx).start()

        @pl.when(t == 1)
        def _():
            def pos_wait(i, _):
                frm = lax.rem(ctx + i, n_ctx)
                remote(pos_in, pos_all.at[frm], pos_send.at[i], pos_recv.at[frm], sibling).wait_recv()
                return 0

            pltpu.make_async_copy(pos_in, pos_all.at[ctx], pos_recv.at[ctx]).wait()
            lax.fori_loop(1, n_ctx, pos_wait, 0)
            q_pos[0] = position_column(2 * w + c)
            q_pos[1] = position_column(2 * mate + c)

        s1, h1 = lax.div(t + heads - 1, heads) - 1, lax.rem(t + heads - 1, heads)

        @pl.when((t > 0) & jnp.logical_not(left_out(h1)))
        def _():
            @pl.when(helper & (t == off + 1))
            def _():
                q_copy().wait_recv()

            @pl.when(w - s1 >= 0)
            def _():
                sib_wait(h1, w - s1)
                attend(h1, w - s1)

            @pl.when((s1 > 0) & (w + s1 < W))
            def _():
                sib_wait(h1, w + s1)
                attend(h1, w + s1)

            @pl.when(s1 == jnp.maximum(w, W - 1 - w))
            def _():
                finish(h1)

        return 0

    lax.fori_loop(0, W * heads + 1, step, 0)

    for h in range(heads):

        @pl.when(crossed | left_out(h))
        def _():
            o_copy(h, 0).wait_recv()

    def product(i, core, j):
        target = 2 * lax.rem(x + i, X) + core
        w_copy(target, j).wait()
        return jnp.dot(normed[...], w_buf[target, j], preferred_element_type=jnp.float32)

    def ps_copy(i, j):
        return remote(part_sib.at[i, j], got_sib.at[i, j], ps_send.at[i, j], ps_recv.at[i, j], sibling)

    def p_copy(i, j):
        to = dev(ctx, 2 * lax.rem(x + i, X) + c)
        return remote(part.at[i - 1, j], got.at[i - 1, j], p_send.at[i - 1, j], p_recv.at[i - 1, j], to)

    def give_sibling(i):
        def body(j, _):
            part_sib[i, j] = product(i, 1 - c, j).astype(jnp.bfloat16)
            ps_copy(i, j).start()
            return 0

        lax.fori_loop(0, n_chunk, body, 0)

    def pair_sum(i, j):
        mine = product(i, c, j)
        ps_copy(i, j).wait_recv()
        return mine + got_sib[i, j].astype(jnp.float32)

    for i in range(1, X):
        give_sibling(i)

        def send_chunk(j, _):
            part[i - 1, j] = pair_sum(i, j).astype(jnp.bfloat16)
            p_copy(i, j).start()
            return 0

        lax.fori_loop(0, n_chunk, send_chunk, 0)
    give_sibling(0)
    res_copy.wait()

    def pos_done(i, _):
        pos_copy(i).wait_send()
        return 0

    lax.fori_loop(1, n_ctx, pos_done, 0)

    @pl.when(crossed)
    def _():
        for h in range(heads):
            for j, (src, dst) in enumerate(init_pairs(h)):
                remote(src, dst, init_send.at[h, j], init_recv.at[h, j], partner).wait_send()

            @pl.when(jnp.logical_not(left_out(h)))
            def _():
                o_copy(h, 0).wait_send()

        for j, (src, dst) in enumerate(small_pairs):
            remote(src, dst, small_send.at[j], small_recv.at[j], partner).wait_send()

    @pl.when(helper)
    def _():
        o_copy(max(off, 0), 1).wait_send()

    @pl.when(at_end)
    def _():
        q_copy().wait_send()

    def line_done(idx, _):
        for h in range(heads):

            @pl.when(jnp.logical_not(left_out(h)))
            def _():
                sib_copy(h, idx).wait_send()

            @pl.when((idx <= w) & goes(1, h) & (jnp.logical_not(left_out(h)) | (idx == w)))
            def _():
                line_copy(h, idx, 1).wait_send()

            @pl.when((idx >= w) & goes(0, h) & (jnp.logical_not(left_out(h)) | (idx == w)))
            def _():
                line_copy(h, idx, 0).wait_send()

        return 0

    lax.fori_loop(0, W, line_done, 0)

    def last_chunk(j, _):
        cols = pl.ds(pl.multiple_of(j * CHUNK, CHUNK), CHUNK)
        result = pair_sum(0, j) + res_buf[:, cols].astype(jnp.float32)
        for i in range(1, X):
            p_copy(i, j).wait()
            result = result + got[i - 1, j].astype(jnp.float32)
        for i in range(X):
            ps_copy(i, j).wait_send()
        out_ref[:, cols] = result.astype(out_ref.dtype)
        return 0

    lax.fori_loop(0, n_chunk, last_chunk, 0)


def per_device(n_ctx, n_tp, queries, keys, values, positions, lambda_vecs, head_gain, out_weight, residual):
    rows = queries.shape[0]
    heads, depth = lambda_vecs.shape[1], lambda_vecs.shape[2]
    wide = 2 * depth
    W, X = n_ctx // 2, n_tp // 2
    columns = out_weight.shape[1] // n_tp
    n_chunk = columns // CHUNK
    vmem = pl.BlockSpec(memory_space=pltpu.VMEM)
    hbm = pl.BlockSpec(memory_space=pl.ANY)
    bf16, f32 = jnp.bfloat16, jnp.float32
    dma = pltpu.SemaphoreType.DMA
    return pl.pallas_call(
        functools.partial(layer_kernel, n_ctx, n_tp),
        out_shape=jax.ShapeDtypeStruct((rows, columns), bf16),
        in_specs=[hbm] * 8,
        out_specs=vmem,
        scratch_shapes=[
            pltpu.VMEM((heads + 1, rows, wide), bf16),
            pltpu.VMEM((heads, W, 2, rows, 2 * wide), bf16),
            pltpu.VMEM((n_ctx, 1, rows), jnp.int32),
            pltpu.VMEM((heads, 4, depth), f32),
            pltpu.VMEM((2 * heads, depth), f32),
            pltpu.VMEM((heads, 1, wide), f32),
            pltpu.VMEM((heads, 1, wide), f32),
            pltpu.VMEM((2, rows, 1), jnp.int32),
            pltpu.VMEM((heads + 1, 2, rows, 1), f32),
            pltpu.VMEM((heads + 1, 2, rows, 1), f32),
            pltpu.VMEM((heads + 1, 2, rows, wide), f32),
            pltpu.VMEM((heads + 1, rows, wide), bf16),
            pltpu.VMEM((rows, heads * wide), bf16),
            pltpu.VMEM((n_tp, n_chunk, heads * wide, CHUNK), bf16),
            pltpu.VMEM((rows, columns), bf16),
            pltpu.VMEM((X, n_chunk, rows, CHUNK), bf16),
            pltpu.VMEM((X, n_chunk, rows, CHUNK), bf16),
            pltpu.VMEM((X - 1, n_chunk, rows, CHUNK), bf16),
            pltpu.VMEM((X - 1, n_chunk, rows, CHUNK), bf16),
            dma((heads, 3)),
            dma((heads, 3)),
            dma((2,)),
            dma((2,)),
            dma((n_ctx,)),
            dma((n_ctx,)),
            dma((2, heads, W)),
            dma((heads, W)),
            dma((heads, W)),
            dma((heads, W)),
            dma(()),
            dma(()),
            dma((heads + 1,)),
            dma((heads,)),
            dma((n_tp, n_chunk)),
            dma(()),
            dma((X, n_chunk)),
            dma((X, n_chunk)),
            dma((X - 1, n_chunk)),
            dma((X - 1, n_chunk)),
        ],
        compiler_params=pltpu.CompilerParams(
            collective_id=0, has_side_effects=True, vmem_limit_bytes=56 * 1024 * 1024
        ),
        name="attend_and_project",
    )(
        queries,
        keys,
        values,
        positions.reshape(1, rows),
        jnp.transpose(lambda_vecs, (1, 0, 2)),
        head_gain.reshape(2 * heads, depth),
        out_weight,
        residual,
    )


def solution(mesh):
    placed = (
        P("ctx", "tp"),
        P("ctx", "tp"),
        P("ctx", "tp"),
        P("ctx"),
        P(None, "tp", None),
        P("tp"),
        P("tp", None),
        P("ctx", "tp"),
    )
    return jax.shard_map(
        functools.partial(per_device, mesh.shape["ctx"], mesh.shape["tp"]),
        mesh=mesh,
        in_specs=placed,
        out_specs=P("ctx", "tp"),
        check_vma=False,
    )
```

time: 62.1 us -> 54.6 us (0.88)
  Pallas kernels: 57.2 us -> 52.7 us
  other arithmetic: 1.92 us -> 0 us
  local copies, waits for them, and re-layouts: 2.61 us -> 1.75 us
    pallas_call x1, Pallas kernels: 57.2 us -> 52.7 us  [per_device(): pl.pallas_call(functools.partial(layer_kernel, n_ctx, n_tp), out_shape=ja...]
    convert_element_type x1 -> x0, other arithmetic: 1.92 us -> none  [per_device(): return (projected + residual.astype(f32)).astype(bf16)]
    reshape x1 -> x0, local copies, waits for them, and re-layouts: 1.31 us -> none  [per_device(): head_gain.reshape(1, heads * wide)]
    unnamed x3 -> x1, local copies, waits for them, and re-layouts: 1.29 us -> 1.75 us
where the time goes in v2:
time: 54.6 us; the launch traced here: 54.4 us
  Pallas kernels  52.7 us (97%)
  local copies, waits for them, and re-layouts  1.75 us (3%)
    pallas_call x1, Pallas kernels, per_device(): pl.pallas_call(functools.partial(layer_kernel, n_ctx, n_tp), out_shape=ja...  52.7 us
    unnamed x1, local copies, waits for them, and re-layouts  1.75 us

profile of v2, /device:TPU:0, one launch (start us, length us, event | category | flops | bytes accessed | tf_op | source)
XLA Modules:
  0.0 54.4 jit_solution(9277751116225541220)
XLA Ops:
  0.0 52.7 %attend_and_project.1 = bf16[144,1280]{1,0:T(8,128)(2,1)} custom-call(bf16[144,768]{1,0:T(8,128)(2,1)} %q_in.1, bf16[144,768]{1,0:T(8,128)(2,1)} %k_in.1, bf16[144,768]{1,0:T(8,128)(2,1)} %v_in.1, s32[1,144]{1,0:T(1,128)} %bitcast.5, f32[3,4,128]{2,1,0:T(4,128)} %bitcast.3, f32[6,128]{1,0:T(8,128)} %bitcast.4, bf16[768,5120]{1,0:T(8,128)(2,1)} %w_in.1, ...), custom_call_target="tpu_custom_call" | custom-call | tf_op jit(solution)/shard_map/attend_and_project/pallas_call | solution.py:484
  52.7 1.7 %copy.10 = bf16[144,1280]{1,0:T(8,128)(2,1)} copy(bf16[144,1280]{1,0:T(8,128)(2,1)} %attend_and_project.1) | data formatting | bytes 737280

commit v3 on v2

--- a/solution.py
+++ b/solution.py
@@ -43,8 +43,6 @@
     normed,
     w_buf,
     res_buf,
-    part_sib,
-    got_sib,
     part,
     got,
     init_send,
@@ -61,10 +59,10 @@
     q_recv,
     o_send,
     o_recv,
-    w_sem,
+    w_local,
+    w_send,
+    w_recv,
     res_sem,
-    ps_send,
-    ps_recv,
     p_send,
     p_recv,
 ):
@@ -74,7 +72,7 @@
     W = n_ctx // 2
     X = n_tp // 2
     n_chunk = w_buf.shape[1]
-    off = heads - 1 if W >= 4 else -1
+    off = 0 if W >= 4 else -1
     scale = 1.0 / math.sqrt(depth)
     ctx = lax.axis_index("ctx")
     tp = lax.axis_index("tp")
@@ -108,6 +106,7 @@
     partner = dev(2 * w + c, 2 * x + y)
     sibling = dev(ctx, 2 * x + 1 - c)
     far = dev(2 * mate + c, 2 * x + y)
+    slant = dev(2 * mate + y, 2 * x + 1 - c)
 
     barrier = pltpu.get_barrier_semaphore()
 
@@ -124,6 +123,10 @@
     def _():
         greet(far)
 
+    @pl.when(at_end | helper)
+    def _():
+        greet(slant)
+
     for i in range(1, X):
         greet(dev(ctx, 2 * lax.rem(x + i, X) + c))
 
@@ -132,7 +135,7 @@
         return 0
 
     lax.fori_loop(1, n_ctx, greet_row, 0)
-    pl.semaphore_wait(barrier, n_ctx - 1 + 1 + X - 1 + lax.rem(c + y, 2) + jnp.where(crossed & (at_end | helper), 1, 0))
+    pl.semaphore_wait(barrier, n_ctx - 1 + 1 + X - 1 + lax.rem(c + y, 2) + jnp.where(at_end | helper, 1 + lax.rem(c + y, 2), 0))
 
     def init_pairs(h):
         cols = pl.ds(h * wide, wide)
@@ -149,6 +152,14 @@
         for h in range(heads):
             for j, (src, dst) in enumerate(init_pairs(h)):
                 pltpu.make_async_copy(src, dst, init_recv.at[h, j]).start()
+            for way in range(2):
+
+                @pl.when(goes(way, h))
+                def _():
+                    to = dev(ctx + (2 if way else -2), tp)
+                    for src, dst in init_pairs(h)[:2]:
+                        remote(src, dst, line_send.at[way, h, w], line_recv.at[h, w], to).start()
+
         for j, (src, dst) in enumerate(small_pairs):
             pltpu.make_async_copy(src, dst, small_recv.at[j]).start()
 
@@ -176,9 +187,33 @@
     pltpu.make_async_copy(pos_in, pos_all.at[ctx], pos_recv.at[ctx]).start()
     lax.fori_loop(1, n_ctx, pos_start, 0)
 
-    def w_copy(i, j):
-        start = pl.multiple_of((i * n_chunk + j) * CHUNK, CHUNK)
-        return pltpu.make_async_copy(w_in.at[:, pl.ds(start, CHUNK)], w_buf.at[i, j], w_sem.at[i, j])
+    col_count = n_chunk * CHUNK
+    w_rows = heads * wide
+
+    def w_src(i, j, core):
+        start = pl.multiple_of((2 * i + core) * col_count + j * CHUNK, CHUNK)
+        return w_in.at[:, pl.ds(start, CHUNK)]
+
+    def w_dst(i, j, group):
+        return w_buf.at[i, j, pl.ds(pl.multiple_of(group * w_rows, 16), w_rows)]
+
+    def w_own(i, j):
+        return pltpu.make_async_copy(w_src(i, j, c), w_dst(i, j, c), w_local.at[i, j])
+
+    def w_give(i, j):
+        return remote(w_src(i, j, 1 - c), w_dst(i, j, c), w_send.at[i, j], w_recv.at[i, j], sibling)
+
+    def w_take(i, j):
+        return remote(w_src(i, j, c), w_dst(i, j, 1 - c), w_send.at[i, j], w_recv.at[i, j], sibling)
+
+    w_total = X * n_chunk
+    w_per_step = -(-w_total // (W * heads - 1))
+
+    def w_start(k, _):
+        i, j = lax.rem(lax.div(k, n_chunk) + x + 1, X), lax.rem(k, n_chunk)
+        w_own(i, j).start()
+        w_give(i, j).start()
+        return 0
 
     res_copy = pltpu.make_async_copy(res_in, res_buf, res_sem)
 
@@ -207,6 +242,11 @@
     def attend(h, idx):
         def one(k, _):
             e = h + k * (heads - h)
+
+            @pl.when((k > 0) & (idx == w))
+            def _():
+                q_copy().wait_recv()
+
             k_pos = jnp.concatenate([pos_all[2 * idx], pos_all[2 * idx + 1]], axis=1)
             allowed = k_pos <= q_pos[k]
             value = kv_buf[h, idx, :, :, pl.ds(wide, wide)].reshape(2 * rows, wide)
@@ -236,13 +276,16 @@
 
         lax.fori_loop(0, slots(h), one, 0)
 
-    def head_columns(h):
-        return pl.ds(pl.multiple_of(h * wide, wide), wide)
-
-    def o_copy(h, k):
+    def head_columns(g, h):
+        return pl.ds(pl.multiple_of((g * heads + h) * wide, wide), wide)
+
+    def o_copy(h, k, core):
         e = h + k * (heads - h)
-        to = dev(2 * (w + k * (mate - w)) + c, 2 * x + y)
-        return remote(stage.at[e], normed.at[:, head_columns(h)], o_send.at[e], o_recv.at[h], to)
+        to = dev(2 * (w + k * (mate - w)) + c, 2 * x + core)
+        return remote(stage.at[e], normed.at[:, head_columns(y, h)], o_send.at[core, e], o_recv.at[y, h], to)
+
+    def o_wait(g, h):
+        remote(stage.at[h], normed.at[:, head_columns(g, h)], o_send.at[0, h], o_recv.at[g, h], sibling).wait_recv()
 
     def finish(h):
         def one(k, _):
@@ -253,22 +296,22 @@
             mean_square = jnp.mean(diff * diff, -1, keepdims=True)
             result = (out_factor * diff * lax.rsqrt(mean_square + norm_eps) * gain_wide[h]).astype(jnp.bfloat16)
 
+            stage[e] = result
+
             @pl.when(straight & (k == 0))
             def _():
-                normed[:, head_columns(h)] = result
-
-            @pl.when(crossed | (k > 0))
-            def _():
-                stage[e] = result
-                o_copy(h, k).start()
+                normed[:, head_columns(y, h)] = result
+
+            for core in range(2):
+
+                @pl.when(crossed | (k > 0) | (c != core))
+                def _():
+                    o_copy(h, k, core).start()
 
             return 0
 
         lax.fori_loop(0, slots(h), one, 0)
 
-    for i in range(1, n_tp + 1):
-        for j in range(n_chunk):
-            w_copy(lax.rem(tp + i, n_tp), j).start()
     res_copy.start()
 
     high[...] = jnp.full(high.shape, LOWEST, jnp.float32)
@@ -287,7 +330,7 @@
 
             for way in range(2):
 
-                @pl.when(goes(way, h))
+                @pl.when(crossed & goes(way, h))
                 def _():
                     line_copy(h, w, way).start()
 
@@ -329,6 +372,10 @@
 
                     sib_copy(h, idx).start()
 
+        lax.fori_loop(
+            jnp.clip((t - 1) * w_per_step, 0, w_total), jnp.clip(t * w_per_step, 0, w_total), w_start, 0
+        )
+
         @pl.when(t == 1)
         def _():
             def pos_wait(i, _):
@@ -345,10 +392,6 @@
 
         @pl.when((t > 0) & jnp.logical_not(left_out(h1)))
         def _():
-            @pl.when(helper & (t == off + 1))
-            def _():
-                q_copy().wait_recv()
-
             @pl.when(w - s1 >= 0)
             def _():
                 sib_wait(h1, w - s1)
@@ -368,47 +411,36 @@
     lax.fori_loop(0, W * heads + 1, step, 0)
 
     for h in range(heads):
-
-        @pl.when(crossed | left_out(h))
-        def _():
-            o_copy(h, 0).wait_recv()
-
-    def product(i, core, j):
-        target = 2 * lax.rem(x + i, X) + core
-        w_copy(target, j).wait()
-        return jnp.dot(normed[...], w_buf[target, j], preferred_element_type=jnp.float32)
-
-    def ps_copy(i, j):
-        return remote(part_sib.at[i, j], got_sib.at[i, j], ps_send.at[i, j], ps_recv.at[i, j], sibling)
+        for g in range(2):
+
+            @pl.when(crossed | (y != g) | left_out(h))
+            def _():
+                o_wait(g, h)
+
+    def product(i, j):
+        w_own(i, j).wait()
+        w_take(i, j).wait_recv()
+        return jnp.dot(normed[...], w_buf[i, j], preferred_element_type=jnp.float32)
 
     def p_copy(i, j):
         to = dev(ctx, 2 * lax.rem(x + i, X) + c)
         return remote(part.at[i - 1, j], got.at[i - 1, j], p_send.at[i - 1, j], p_recv.at[i - 1, j], to)
 
-    def give_sibling(i):
-        def body(j, _):
-            part_sib[i, j] = product(i, 1 - c, j).astype(jnp.bfloat16)
-            ps_copy(i, j).start()
-            return 0
-
-        lax.fori_loop(0, n_chunk, body, 0)
-
-    def pair_sum(i, j):
-        mine = product(i, c, j)
-        ps_copy(i, j).wait_recv()
-        return mine + got_sib[i, j].astype(jnp.float32)
-
     for i in range(1, X):
-        give_sibling(i)
 
         def send_chunk(j, _):
-            part[i - 1, j] = pair_sum(i, j).astype(jnp.bfloat16)
+            part[i - 1, j] = product(lax.rem(x + i, X), j).astype(jnp.bfloat16)
             p_copy(i, j).start()
             return 0
 
         lax.fori_loop(0, n_chunk, send_chunk, 0)
-    give_sibling(0)
     res_copy.wait()
+
+    def w_done(k, _):
+        w_give(lax.div(k, n_chunk), lax.rem(k, n_chunk)).wait_send()
+        return 0
+
+    lax.fori_loop(0, w_total, w_done, 0)
 
     def pos_done(i, _):
         pos_copy(i).wait_send()
@@ -424,14 +456,24 @@
 
             @pl.when(jnp.logical_not(left_out(h)))
             def _():
-                o_copy(h, 0).wait_send()
+                o_copy(h, 0, 1 - c).wait_send()
+                o_copy(h, 0, c).wait_send()
 
         for j, (src, dst) in enumerate(small_pairs):
             remote(src, dst, small_send.at[j], small_recv.at[j], partner).wait_send()
 
+    @pl.when(straight)
+    def _():
+        for h in range(heads):
+
+            @pl.when(jnp.logical_not(left_out(h)))
+            def _():
+                o_copy(h, 0, 1 - c).wait_send()
+
     @pl.when(helper)
     def _():
-        o_copy(max(off, 0), 1).wait_send()
+        for core in range(2):
+            o_copy(max(off, 0), 1, core).wait_send()
 
     @pl.when(at_end)
     def _():
@@ -458,12 +500,10 @@
 
     def last_chunk(j, _):
         cols = pl.ds(pl.multiple_of(j * CHUNK, CHUNK), CHUNK)
-        result = pair_sum(0, j) + res_buf[:, cols].astype(jnp.float32)
+        result = product(x, j) + res_buf[:, cols].astype(jnp.float32)
         for i in range(1, X):
             p_copy(i, j).wait()
             result = result + got[i - 1, j].astype(jnp.float32)
-        for i in range(X):
-            ps_copy(i, j).wait_send()
         out_ref[:, cols] = result.astype(out_ref.dtype)
         return 0
 
@@ -499,11 +539,9 @@
             pltpu.VMEM((heads + 1, 2, rows, 1), f32),
             pltpu.VMEM((heads + 1, 2, rows, wide), f32),
             pltpu.VMEM((heads + 1, rows, wide), bf16),
-            pltpu.VMEM((rows, heads * wide), bf16),
-            pltpu.VMEM((n_tp, n_chunk, heads * wide, CHUNK), bf16),
+            pltpu.VMEM((rows, 2 * heads * wide), bf16),
+            pltpu.VMEM((X, n_chunk, 2 * heads * wide, CHUNK), bf16),
             pltpu.VMEM((rows, columns), bf16),
-            pltpu.VMEM((X, n_chunk, rows, CHUNK), bf16),
-            pltpu.VMEM((X, n_chunk, rows, CHUNK), bf16),
             pltpu.VMEM((X - 1, n_chunk, rows, CHUNK), bf16),
             pltpu.VMEM((X - 1, n_chunk, rows, CHUNK), bf16),
             dma((heads, 3)),
@@ -518,12 +556,12 @@
             dma((heads, W)),
             dma(()),
             dma(()),
-            dma((heads + 1,)),
-            dma((heads,)),
-            dma((n_tp, n_chunk)),
-            dma(()),
+            dma((2, heads + 1)),
+            dma((2, heads)),
             dma((X, n_chunk)),
             dma((X, n_chunk)),
+            dma((X, n_chunk)),
+            dma(()),
             dma((X - 1, n_chunk)),
             dma((X - 1, n_chunk)),
         ],

time: 54.6 us -> 59.9 us (1.097)
  Pallas kernels: 52.7 us -> 57.9 us
    pallas_call x1, Pallas kernels: 52.7 us -> 57.9 us  [per_device(): pl.pallas_call(functools.partial(layer_kernel, n_ctx, n_tp), out_shape=ja...]
where the time goes in v3:
time: 59.9 us; the launch traced here: 59.7 us
  Pallas kernels  57.9 us (97%)
  local copies, waits for them, and re-layouts  1.75 us (3%)
    pallas_call x1, Pallas kernels, per_device(): pl.pallas_call(functools.partial(layer_kernel, n_ctx, n_tp), out_shape=ja...  57.9 us
    unnamed x1, local copies, waits for them, and re-layouts  1.75 us

profile of v3, /device:TPU:0, one launch (start us, length us, event | category | flops | bytes accessed | tf_op | source)
XLA Modules:
  0.0 59.7 jit_solution(11038718287121675014)
XLA Ops:
  0.0 57.9 %attend_and_project.1 = bf16[144,1280]{1,0:T(8,128)(2,1)} custom-call(bf16[144,768]{1,0:T(8,128)(2,1)} %q_in.1, bf16[144,768]{1,0:T(8,128)(2,1)} %k_in.1, bf16[144,768]{1,0:T(8,128)(2,1)} %v_in.1, s32[1,144]{1,0:T(1,128)} %bitcast.5, f32[3,4,128]{2,1,0:T(4,128)} %bitcast.3, f32[6,128]{1,0:T(8,128)} %bitcast.4, bf16[768,5120]{1,0:T(8,128)(2,1)} %w_in.1, ...), custom_call_target="tpu_custom_call" | custom-call | tf_op jit(solution)/shard_map/attend_and_project/pallas_call | solution.py:524
  58.0 1.7 %copy.10 = bf16[144,1280]{1,0:T(8,128)(2,1)} copy(bf16[144,1280]{1,0:T(8,128)(2,1)} %attend_and_project.1) | data formatting | bytes 737280

commit v4 on v2

--- a/solution.py
+++ b/solution.py
@@ -75,7 +75,7 @@
     X = n_tp // 2
     n_chunk = w_buf.shape[1]
     off = heads - 1 if W >= 4 else -1
-    scale = 1.0 / math.sqrt(depth)
+    scale = math.log2(math.e) / math.sqrt(depth)
     ctx = lax.axis_index("ctx")
     tp = lax.axis_index("tp")
     w, y = lax.div(ctx, 2), lax.rem(ctx, 2)
@@ -149,6 +149,14 @@
         for h in range(heads):
             for j, (src, dst) in enumerate(init_pairs(h)):
                 pltpu.make_async_copy(src, dst, init_recv.at[h, j]).start()
+            for way in range(2):
+
+                @pl.when(goes(way, h))
+                def _():
+                    to = dev(ctx + (2 if way else -2), tp)
+                    for src, dst in init_pairs(h)[:2]:
+                        remote(src, dst, line_send.at[way, h, w], line_recv.at[h, w], to).start()
+
         for j, (src, dst) in enumerate(small_pairs):
             pltpu.make_async_copy(src, dst, small_recv.at[j]).start()
 
@@ -180,6 +188,14 @@
         start = pl.multiple_of((i * n_chunk + j) * CHUNK, CHUNK)
         return pltpu.make_async_copy(w_in.at[:, pl.ds(start, CHUNK)], w_buf.at[i, j], w_sem.at[i, j])
 
+    w_total = n_tp * n_chunk
+    w_per_step = -(-w_total // (W * heads - 1))
+
+    def w_start(k, _):
+        i, core = lax.rem(lax.div(k, 2 * n_chunk) + x + 1, X), lax.rem(lax.div(k, n_chunk) + c + 1, 2)
+        w_copy(2 * i + core, lax.rem(k, n_chunk)).start()
+        return 0
+
     res_copy = pltpu.make_async_copy(res_in, res_buf, res_sem)
 
     def line_copy(h, idx, way):
@@ -204,34 +220,37 @@
         same = lax.broadcasted_iota(jnp.int32, square, 0) == lax.broadcasted_iota(jnp.int32, square, 1)
         return jnp.sum(jnp.where(same, jnp.broadcast_to(line, square), 0), -1, keepdims=True)
 
-    def attend(h, idx):
+    def attend(h, blocks):
         def one(k, _):
             e = h + k * (heads - h)
-            k_pos = jnp.concatenate([pos_all[2 * idx], pos_all[2 * idx + 1]], axis=1)
-            allowed = k_pos <= q_pos[k]
-            value = kv_buf[h, idx, :, :, pl.ds(wide, wide)].reshape(2 * rows, wide)
-            before = [high[e, a] for a in range(2)]
-            sums = [total[e, a] for a in range(2)]
-            held = [acc[e, a] for a in range(2)]
+            allowed = [
+                jnp.concatenate([pos_all[2 * idx], pos_all[2 * idx + 1]], axis=1) <= q_pos[k] for idx in blocks
+            ]
+            values = [kv_buf[h, idx, :, :, pl.ds(wide, wide)].reshape(2 * rows, wide) for idx in blocks]
+            fresh = []
             for a in range(2):
                 query = q_buf[e, :, pl.ds(a * depth, depth)]
-                key = kv_buf[h, idx, :, :, pl.ds(a * depth, depth)].reshape(2 * rows, depth)
-                scores = (
-                    lax.dot_general(query, key, (((1,), (1,)), ((), ())), preferred_element_type=jnp.float32) * scale
-                )
-                scores = jnp.where(allowed, scores, MASKED)
-                now = jnp.maximum(before[a], jnp.max(scores, -1, keepdims=True))
-                keep = jnp.exp(before[a] - now)
-                expo = jnp.exp(scores - now)
-                before[a] = now
-                sums[a] = sums[a] * keep + jnp.sum(expo, -1, keepdims=True)
-                held[a] = held[a] * keep + jnp.dot(
-                    expo.astype(jnp.bfloat16), value, preferred_element_type=jnp.float32
-                )
+                scores = []
+                for idx, mask in zip(blocks, allowed):
+                    key = kv_buf[h, idx, :, :, pl.ds(a * depth, depth)].reshape(2 * rows, depth)
+                    raw = lax.dot_general(
+                        query, key, (((1,), (1,)), ((), ())), preferred_element_type=jnp.float32
+                    )
+                    scores.append(jnp.where(mask, raw, MASKED))
+                before = high[e, a]
+                now = before
+                for part_scores in scores:
+                    now = jnp.maximum(now, jnp.max(part_scores, -1, keepdims=True))
+                keep = jnp.exp2((before - now) * scale)
+                sums = total[e, a] * keep
+                held = acc[e, a] * jnp.concatenate([keep] * (wide // 128), axis=1)
+                for part_scores, value in zip(scores, values):
+                    expo = jnp.exp2((part_scores - now[:, :1]) * scale)
+                    sums = sums + jnp.sum(expo, -1, keepdims=True)
+                    held = held + jnp.dot(expo.astype(jnp.bfloat16), value, preferred_element_type=jnp.float32)
+                fresh.append((now, sums, held))
             for a in range(2):
-                high[e, a] = before[a]
-                total[e, a] = sums[a]
-                acc[e, a] = held[a]
+                high[e, a], total[e, a], acc[e, a] = fresh[a]
             return 0
 
         lax.fori_loop(0, slots(h), one, 0)
@@ -247,8 +266,8 @@
     def finish(h):
         def one(k, _):
             e = h + k * (heads - h)
-            first = acc[e, 0] / total[e, 0]
-            second = acc[e, 1] / total[e, 1]
+            first = acc[e, 0] / total[e, 0, :, :1]
+            second = acc[e, 1] / total[e, 1, :, :1]
             diff = first - lam_wide[h] * second
             mean_square = jnp.mean(diff * diff, -1, keepdims=True)
             result = (out_factor * diff * lax.rsqrt(mean_square + norm_eps) * gain_wide[h]).astype(jnp.bfloat16)
@@ -266,9 +285,6 @@
 
         lax.fori_loop(0, slots(h), one, 0)
 
-    for i in range(1, n_tp + 1):
-        for j in range(n_chunk):
-            w_copy(lax.rem(tp + i, n_tp), j).start()
     res_copy.start()
 
     high[...] = jnp.full(high.shape, LOWEST, jnp.float32)
@@ -287,7 +303,7 @@
 
             for way in range(2):
 
-                @pl.when(goes(way, h))
+                @pl.when(crossed & goes(way, h))
                 def _():
                     line_copy(h, w, way).start()
 
@@ -329,6 +345,10 @@
 
                     sib_copy(h, idx).start()
 
+        lax.fori_loop(
+            jnp.clip((t - 1) * w_per_step, 0, w_total), jnp.clip(t * w_per_step, 0, w_total), w_start, 0
+        )
+
         @pl.when(t == 1)
         def _():
             def pos_wait(i, _):
@@ -338,8 +358,8 @@
 
             pltpu.make_async_copy(pos_in, pos_all.at[ctx], pos_recv.at[ctx]).wait()
             lax.fori_loop(1, n_ctx, pos_wait, 0)
-            q_pos[0] = position_column(2 * w + c)
-            q_pos[1] = position_column(2 * mate + c)
+            q_pos[0] = jnp.broadcast_to(position_column(2 * w + c), q_pos.shape[1:])
+            q_pos[1] = jnp.broadcast_to(position_column(2 * mate + c), q_pos.shape[1:])
 
         s1, h1 = lax.div(t + heads - 1, heads) - 1, lax.rem(t + heads - 1, heads)
 
@@ -349,15 +369,19 @@
             def _():
                 q_copy().wait_recv()
 
-            @pl.when(w - s1 >= 0)
+            on_left, on_right = w - s1 >= 0, (s1 > 0) & (w + s1 < W)
+
+            @pl.when(on_left & on_right)
             def _():
                 sib_wait(h1, w - s1)
-                attend(h1, w - s1)
-
-            @pl.when((s1 > 0) & (w + s1 < W))
-            def _():
                 sib_wait(h1, w + s1)
-                attend(h1, w + s1)
+                attend(h1, (w - s1, w + s1))
+
+            @pl.when(on_left != on_right)
+            def _():
+                idx = jnp.where(on_left, w - s1, w + s1)
+                sib_wait(h1, idx)
+                attend(h1, (idx,))
 
             @pl.when(s1 == jnp.maximum(w, W - 1 - w))
             def _():
@@ -399,14 +423,21 @@
         return mine + got_sib[i, j].astype(jnp.float32)
 
     for i in range(1, X):
-        give_sibling(i)
 
         def send_chunk(j, _):
-            part[i - 1, j] = pair_sum(i, j).astype(jnp.bfloat16)
-            p_copy(i, j).start()
+            @pl.when(j < n_chunk)
+            def _():
+                part_sib[i, j] = product(i, 1 - c, j).astype(jnp.bfloat16)
+                ps_copy(i, j).start()
+
+            @pl.when(j >= 2)
+            def _():
+                part[i - 1, j - 2] = pair_sum(i, j - 2).astype(jnp.bfloat16)
+                p_copy(i, j - 2).start()
+
             return 0
 
-        lax.fori_loop(0, n_chunk, send_chunk, 0)
+        lax.fori_loop(0, n_chunk + 2, send_chunk, 0)
     give_sibling(0)
     res_copy.wait()
 
@@ -494,9 +525,9 @@
             pltpu.VMEM((2 * heads, depth), f32),
             pltpu.VMEM((heads, 1, wide), f32),
             pltpu.VMEM((heads, 1, wide), f32),
-            pltpu.VMEM((2, rows, 1), jnp.int32),
-            pltpu.VMEM((heads + 1, 2, rows, 1), f32),
-            pltpu.VMEM((heads + 1, 2, rows, 1), f32),
+            pltpu.VMEM((2, rows, 2 * rows), jnp.int32),
+            pltpu.VMEM((heads + 1, 2, rows, 128), f32),
+            pltpu.VMEM((heads + 1, 2, rows, 128), f32),
             pltpu.VMEM((heads + 1, 2, rows, wide), f32),
             pltpu.VMEM((heads + 1, rows, wide), bf16),
             pltpu.VMEM((rows, heads * wide), bf16),

time: 54.6 us -> 53.6 us (0.982)
  Pallas kernels: 52.7 us -> 51.7 us
    pallas_call x1, Pallas kernels: 52.7 us -> 51.7 us  [per_device(): pl.pallas_call(functools.partial(layer_kernel, n_ctx, n_tp), out_shape=ja...]
where the time goes in v4:
time: 53.6 us; the launch traced here: 53.4 us
  Pallas kernels  51.7 us (96%)
  local copies, waits for them, and re-layouts  1.75 us (3%)
    pallas_call x1, Pallas kernels, per_device(): pl.pallas_call(functools.partial(layer_kernel, n_ctx, n_tp), out_shape=ja...  51.7 us
    unnamed x1, local copies, waits for them, and re-layouts  1.75 us

profile of v4, /device:TPU:0, one launch (start us, length us, event | category | flops | bytes accessed | tf_op | source)
XLA Modules:
  0.0 53.4 jit_solution(8993842941880488419)
XLA Ops:
  0.0 51.7 %attend_and_project.1 = bf16[144,1280]{1,0:T(8,128)(2,1)} custom-call(bf16[144,768]{1,0:T(8,128)(2,1)} %q_in.1, bf16[144,768]{1,0:T(8,128)(2,1)} %k_in.1, bf16[144,768]{1,0:T(8,128)(2,1)} %v_in.1, s32[1,144]{1,0:T(1,128)} %bitcast.5, f32[3,4,128]{2,1,0:T(4,128)} %bitcast.3, f32[6,128]{1,0:T(8,128)} %bitcast.4, bf16[768,5120]{1,0:T(8,128)(2,1)} %w_in.1, ...), custom_call_target="tpu_custom_call" | custom-call | tf_op jit(solution)/shard_map/attend_and_project/pallas_call | solution.py:515
  51.7 1.7 %copy.10 = bf16[144,1280]{1,0:T(8,128)(2,1)} copy(bf16[144,1280]{1,0:T(8,128)(2,1)} %attend_and_project.1) | data formatting | bytes 737280

commit v5 on v4

--- a/solution.py
+++ b/solution.py
@@ -42,6 +42,7 @@
     stage,
     normed,
     w_buf,
+    w_sib,
     res_buf,
     part_sib,
     got_sib,
@@ -62,6 +63,8 @@
     o_send,
     o_recv,
     w_sem,
+    ws_send,
+    ws_recv,
     res_sem,
     ps_send,
     ps_recv,
@@ -108,6 +111,7 @@
     partner = dev(2 * w + c, 2 * x + y)
     sibling = dev(ctx, 2 * x + 1 - c)
     far = dev(2 * mate + c, 2 * x + y)
+    slant = dev(2 * mate + y, 2 * x + 1 - c)
 
     barrier = pltpu.get_barrier_semaphore()
 
@@ -124,6 +128,10 @@
     def _():
         greet(far)
 
+    @pl.when(at_end | helper)
+    def _():
+        greet(slant)
+
     for i in range(1, X):
         greet(dev(ctx, 2 * lax.rem(x + i, X) + c))
 
@@ -132,7 +140,7 @@
         return 0
 
     lax.fori_loop(1, n_ctx, greet_row, 0)
-    pl.semaphore_wait(barrier, n_ctx - 1 + 1 + X - 1 + lax.rem(c + y, 2) + jnp.where(crossed & (at_end | helper), 1, 0))
+    pl.semaphore_wait(barrier, n_ctx - 1 + 1 + X - 1 + lax.rem(c + y, 2) + jnp.where(at_end | helper, 1 + lax.rem(c + y, 2), 0))
 
     def init_pairs(h):
         cols = pl.ds(h * wide, wide)
@@ -188,12 +196,24 @@
         start = pl.multiple_of((i * n_chunk + j) * CHUNK, CHUNK)
         return pltpu.make_async_copy(w_in.at[:, pl.ds(start, CHUNK)], w_buf.at[i, j], w_sem.at[i, j])
 
-    w_total = n_tp * n_chunk
+    w_total = (X + 1) * n_chunk
     w_per_step = -(-w_total // (W * heads - 1))
 
     def w_start(k, _):
-        i, core = lax.rem(lax.div(k, 2 * n_chunk) + x + 1, X), lax.rem(lax.div(k, n_chunk) + c + 1, 2)
-        w_copy(2 * i + core, lax.rem(k, n_chunk)).start()
+        m = lax.div(k, n_chunk)
+        i, core = jnp.where(m < X - 1, m + 1, 0), jnp.where(m == X - 1, 1 - c, c)
+        w_copy(2 * lax.rem(x + i, X) + core, lax.rem(k, n_chunk)).start()
+        return 0
+
+    ws_total = (X - 1) * n_chunk
+    ws_per_step = -(-ws_total // (W * heads - 2))
+
+    def ws_copy(i, j, core):
+        start = pl.multiple_of(((2 * lax.rem(x + i + 1, X) + core) * n_chunk + j) * CHUNK, CHUNK)
+        return remote(w_in.at[:, pl.ds(start, CHUNK)], w_sib.at[i, j], ws_send.at[i, j], ws_recv.at[i, j], sibling)
+
+    def ws_start(k, _):
+        ws_copy(lax.div(k, n_chunk), lax.rem(k, n_chunk), 1 - c).start()
         return 0
 
     res_copy = pltpu.make_async_copy(res_in, res_buf, res_sem)
@@ -220,8 +240,9 @@
         same = lax.broadcasted_iota(jnp.int32, square, 0) == lax.broadcasted_iota(jnp.int32, square, 1)
         return jnp.sum(jnp.where(same, jnp.broadcast_to(line, square), 0), -1, keepdims=True)
 
-    def attend(h, blocks):
-        def one(k, _):
+    def attend(h, blocks, last):
+        def one(turn, _):
+            k = slots(h) - 1 - turn
             e = h + k * (heads - h)
             allowed = [
                 jnp.concatenate([pos_all[2 * idx], pos_all[2 * idx + 1]], axis=1) <= q_pos[k] for idx in blocks
@@ -251,6 +272,11 @@
                 fresh.append((now, sums, held))
             for a in range(2):
                 high[e, a], total[e, a], acc[e, a] = fresh[a]
+
+            @pl.when(last)
+            def _():
+                finish(h, k)
+
             return 0
 
         lax.fori_loop(0, slots(h), one, 0)
@@ -258,32 +284,32 @@
     def head_columns(h):
         return pl.ds(pl.multiple_of(h * wide, wide), wide)
 
-    def o_copy(h, k):
+    def o_copy(h, k, core):
         e = h + k * (heads - h)
-        to = dev(2 * (w + k * (mate - w)) + c, 2 * x + y)
-        return remote(stage.at[e], normed.at[:, head_columns(h)], o_send.at[e], o_recv.at[h], to)
-
-    def finish(h):
-        def one(k, _):
-            e = h + k * (heads - h)
-            first = acc[e, 0] / total[e, 0, :, :1]
-            second = acc[e, 1] / total[e, 1, :, :1]
-            diff = first - lam_wide[h] * second
-            mean_square = jnp.mean(diff * diff, -1, keepdims=True)
-            result = (out_factor * diff * lax.rsqrt(mean_square + norm_eps) * gain_wide[h]).astype(jnp.bfloat16)
-
-            @pl.when(straight & (k == 0))
-            def _():
-                normed[:, head_columns(h)] = result
-
-            @pl.when(crossed | (k > 0))
-            def _():
-                stage[e] = result
-                o_copy(h, k).start()
-
-            return 0
-
-        lax.fori_loop(0, slots(h), one, 0)
+        to = dev(2 * (w + k * (mate - w)) + c, 2 * x + core)
+        return remote(stage.at[e], normed.at[y, :, head_columns(h)], o_send.at[core, e], o_recv.at[y, h], to)
+
+    def o_wait(g, h):
+        remote(stage.at[h], normed.at[g, :, head_columns(h)], o_send.at[0, h], o_recv.at[g, h], sibling).wait_recv()
+
+    def finish(h, k):
+        e = h + k * (heads - h)
+        first = acc[e, 0] / total[e, 0, :, :1]
+        second = acc[e, 1] / total[e, 1, :, :1]
+        diff = first - lam_wide[h] * second
+        mean_square = jnp.mean(diff * diff, -1, keepdims=True)
+        result = (out_factor * diff * lax.rsqrt(mean_square + norm_eps) * gain_wide[h]).astype(jnp.bfloat16)
+        stage[e] = result
+
+        @pl.when(straight & (k == 0))
+        def _():
+            normed[y, :, head_columns(h)] = result
+
+        for core in range(2):
+
+            @pl.when(crossed | (k > 0) | (c != core))
+            def _():
+                o_copy(h, k, core).start()
 
     res_copy.start()
 
@@ -349,6 +375,10 @@
             jnp.clip((t - 1) * w_per_step, 0, w_total), jnp.clip(t * w_per_step, 0, w_total), w_start, 0
         )
 
+        lax.fori_loop(
+            jnp.clip((t - 1) * ws_per_step, 0, ws_total), jnp.clip(t * ws_per_step, 0, ws_total), ws_start, 0
+        )
+
         @pl.when(t == 1)
         def _():
             def pos_wait(i, _):
@@ -369,77 +399,68 @@
             def _():
                 q_copy().wait_recv()
 
+            last = s1 == jnp.maximum(w, W - 1 - w)
             on_left, on_right = w - s1 >= 0, (s1 > 0) & (w + s1 < W)
 
             @pl.when(on_left & on_right)
             def _():
                 sib_wait(h1, w - s1)
                 sib_wait(h1, w + s1)
-                attend(h1, (w - s1, w + s1))
+                attend(h1, (w - s1, w + s1), last)
 
             @pl.when(on_left != on_right)
             def _():
                 idx = jnp.where(on_left, w - s1, w + s1)
                 sib_wait(h1, idx)
-                attend(h1, (idx,))
-
-            @pl.when(s1 == jnp.maximum(w, W - 1 - w))
-            def _():
-                finish(h1)
+                attend(h1, (idx,), last)
 
         return 0
 
     lax.fori_loop(0, W * heads + 1, step, 0)
 
     for h in range(heads):
-
-        @pl.when(crossed | left_out(h))
-        def _():
-            o_copy(h, 0).wait_recv()
+        for g in range(2):
+
+            @pl.when(crossed | (y != g) | left_out(h))
+            def _():
+                o_wait(g, h)
 
     def product(i, core, j):
         target = 2 * lax.rem(x + i, X) + core
         w_copy(target, j).wait()
-        return jnp.dot(normed[...], w_buf[target, j], preferred_element_type=jnp.float32)
-
-    def ps_copy(i, j):
-        return remote(part_sib.at[i, j], got_sib.at[i, j], ps_send.at[i, j], ps_recv.at[i, j], sibling)
+        return jnp.dot(normed[c], w_buf[target, j], preferred_element_type=jnp.float32)
+
+    def ps_copy(j):
+        return remote(part_sib.at[j], got_sib.at[j], ps_send.at[j], ps_recv.at[j], sibling)
 
     def p_copy(i, j):
         to = dev(ctx, 2 * lax.rem(x + i, X) + c)
         return remote(part.at[i - 1, j], got.at[i - 1, j], p_send.at[i - 1, j], p_recv.at[i - 1, j], to)
 
-    def give_sibling(i):
-        def body(j, _):
-            part_sib[i, j] = product(i, 1 - c, j).astype(jnp.bfloat16)
-            ps_copy(i, j).start()
+    for i in range(1, X):
+
+        def send_chunk(j, _):
+            ws_copy(i - 1, j, c).wait_recv()
+            both = product(i, c, j) + jnp.dot(normed[1 - c], w_sib[i - 1, j], preferred_element_type=jnp.float32)
+            part[i - 1, j] = both.astype(jnp.bfloat16)
+            p_copy(i, j).start()
             return 0
 
-        lax.fori_loop(0, n_chunk, body, 0)
-
-    def pair_sum(i, j):
-        mine = product(i, c, j)
-        ps_copy(i, j).wait_recv()
-        return mine + got_sib[i, j].astype(jnp.float32)
-
-    for i in range(1, X):
-
-        def send_chunk(j, _):
-            @pl.when(j < n_chunk)
-            def _():
-                part_sib[i, j] = product(i, 1 - c, j).astype(jnp.bfloat16)
-                ps_copy(i, j).start()
-
-            @pl.when(j >= 2)
-            def _():
-                part[i - 1, j - 2] = pair_sum(i, j - 2).astype(jnp.bfloat16)
-                p_copy(i, j - 2).start()
-
-            return 0
-
-        lax.fori_loop(0, n_chunk + 2, send_chunk, 0)
-    give_sibling(0)
+        lax.fori_loop(0, n_chunk, send_chunk, 0)
+
+    def give_sibling(j, _):
+        part_sib[j] = product(0, 1 - c, j).astype(jnp.bfloat16)
+        ps_copy(j).start()
+        return 0
+
+    lax.fori_loop(0, n_chunk, give_sibling, 0)
     res_copy.wait()
+
+    def ws_done(k, _):
+        ws_copy(lax.div(k, n_chunk), lax.rem(k, n_chunk), 1 - c).wait_send()
+        return 0
+
+    lax.fori_loop(0, ws_total, ws_done, 0)
 
     def pos_done(i, _):
         pos_copy(i).wait_send()
@@ -455,14 +476,24 @@
 
             @pl.when(jnp.logical_not(left_out(h)))
             def _():
-                o_copy(h, 0).wait_send()
+                o_copy(h, 0, 1 - c).wait_send()
+                o_copy(h, 0, c).wait_send()
 
         for j, (src, dst) in enumerate(small_pairs):
             remote(src, dst, small_send.at[j], small_recv.at[j], partner).wait_send()
 
+    @pl.when(straight)
+    def _():
+        for h in range(heads):
+
+            @pl.when(jnp.logical_not(left_out(h)))
+            def _():
+                o_copy(h, 0, 1 - c).wait_send()
+
     @pl.when(helper)
     def _():
-        o_copy(max(off, 0), 1).wait_send()
+        for core in range(2):
+            o_copy(max(off, 0), 1, core).wait_send()
 
     @pl.when(at_end)
     def _():
@@ -489,12 +520,12 @@
 
     def last_chunk(j, _):
         cols = pl.ds(pl.multiple_of(j * CHUNK, CHUNK), CHUNK)
-        result = pair_sum(0, j) + res_buf[:, cols].astype(jnp.float32)
+        mine = product(0, c, j) + res_buf[:, cols].astype(jnp.float32)
+        ps_copy(j).wait()
+        result = mine + got_sib[j].astype(jnp.float32)
         for i in range(1, X):
             p_copy(i, j).wait()
             result = result + got[i - 1, j].astype(jnp.float32)
-        for i in range(X):
-            ps_copy(i, j).wait_send()
         out_ref[:, cols] = result.astype(out_ref.dtype)
         return 0
 
@@ -530,11 +561,12 @@
             pltpu.VMEM((heads + 1, 2, rows, 128), f32),
             pltpu.VMEM((heads + 1, 2, rows, wide), f32),
             pltpu.VMEM((heads + 1, rows, wide), bf16),
-            pltpu.VMEM((rows, heads * wide), bf16),
+            pltpu.VMEM((2, rows, heads * wide), bf16),
             pltpu.VMEM((n_tp, n_chunk, heads * wide, CHUNK), bf16),
+            pltpu.VMEM((X - 1, n_chunk, heads * wide, CHUNK), bf16),
             pltpu.VMEM((rows, columns), bf16),
-            pltpu.VMEM((X, n_chunk, rows, CHUNK), bf16),
-            pltpu.VMEM((X, n_chunk, rows, CHUNK), bf16),
+            pltpu.VMEM((n_chunk, rows, CHUNK), bf16),
+            pltpu.VMEM((n_chunk, rows, CHUNK), bf16),
             pltpu.VMEM((X - 1, n_chunk, rows, CHUNK), bf16),
             pltpu.VMEM((X - 1, n_chunk, rows, CHUNK), bf16),
             dma((heads, 3)),
@@ -549,12 +581,14 @@
             dma((heads, W)),
             dma(()),
             dma(()),
-            dma((heads + 1,)),
-            dma((heads,)),
+            dma((2, heads + 1)),
+            dma((2, heads)),
             dma((n_tp, n_chunk)),
+            dma((X - 1, n_chunk)),
+            dma((X - 1, n_chunk)),
             dma(()),
-            dma((X, n_chunk)),
-            dma((X, n_chunk)),
+            dma((n_chunk,)),
+            dma((n_chunk,)),
             dma((X - 1, n_chunk)),
             dma((X - 1, n_chunk)),
         ],

time: 53.6 us -> 54.9 us (1.024)
  Pallas kernels: 51.7 us -> 52.9 us
    pallas_call x1, Pallas kernels: 51.7 us -> 52.9 us  [per_device(): pl.pallas_call(functools.partial(layer_kernel, n_ctx, n_tp), out_shape=ja...]
where the time goes in v5:
time: 54.9 us; the launch traced here: 54.7 us
  Pallas kernels  52.9 us (96%)
  local copies, waits for them, and re-layouts  1.75 us (3%)
    pallas_call x1, Pallas kernels, per_device(): pl.pallas_call(functools.partial(layer_kernel, n_ctx, n_tp), out_shape=ja...  52.9 us
    unnamed x1, local copies, waits for them, and re-layouts  1.75 us

profile of v5, /device:TPU:0, one launch (start us, length us, event | category | flops | bytes accessed | tf_op | source)
XLA Modules:
  0.0 54.7 jit_solution(6908640968569876763)
XLA Ops:
  0.0 52.9 %attend_and_project.1 = bf16[144,1280]{1,0:T(8,128)(2,1)} custom-call(bf16[144,768]{1,0:T(8,128)(2,1)} %q_in.1, bf16[144,768]{1,0:T(8,128)(2,1)} %k_in.1, bf16[144,768]{1,0:T(8,128)(2,1)} %v_in.1, s32[1,144]{1,0:T(1,128)} %bitcast.5, f32[3,4,128]{2,1,0:T(4,128)} %bitcast.3, f32[6,128]{1,0:T(8,128)} %bitcast.4, bf16[768,5120]{1,0:T(8,128)(2,1)} %w_in.1, ...), custom_call_target="tpu_custom_call" | custom-call | tf_op jit(solution)/shard_map/attend_and_project/pallas_call | solution.py:546
  52.9 1.7 %copy.10 = bf16[144,1280]{1,0:T(8,128)(2,1)} copy(bf16[144,1280]{1,0:T(8,128)(2,1)} %attend_and_project.1) | data formatting | bytes 737280

commit v6 on v4

--- a/solution.py
+++ b/solution.py
@@ -144,27 +144,27 @@
 
     small_pairs = ((lam_in, lam_buf), (gain_in, gain_buf))
 
+    def init_start(h):
+        @pl.when(straight)
+        def _():
+            for j, (src, dst) in enumerate(init_pairs(h)):
+                pltpu.make_async_copy(src, dst, init_recv.at[h, j]).start()
+
+        @pl.when(crossed)
+        def _():
+            for j, (src, dst) in enumerate(init_pairs(h)):
+                remote(src, dst, init_send.at[h, j], init_recv.at[h, j], partner).start()
+
+    for h in range(min(2, heads)):
+        init_start(h)
+
     @pl.when(straight)
     def _():
-        for h in range(heads):
-            for j, (src, dst) in enumerate(init_pairs(h)):
-                pltpu.make_async_copy(src, dst, init_recv.at[h, j]).start()
-            for way in range(2):
-
-                @pl.when(goes(way, h))
-                def _():
-                    to = dev(ctx + (2 if way else -2), tp)
-                    for src, dst in init_pairs(h)[:2]:
-                        remote(src, dst, line_send.at[way, h, w], line_recv.at[h, w], to).start()
-
         for j, (src, dst) in enumerate(small_pairs):
             pltpu.make_async_copy(src, dst, small_recv.at[j]).start()
 
     @pl.when(crossed)
     def _():
-        for h in range(heads):
-            for j, (src, dst) in enumerate(init_pairs(h)):
-                remote(src, dst, init_send.at[h, j], init_recv.at[h, j], partner).start()
         for j, (src, dst) in enumerate(small_pairs):
             remote(src, dst, small_send.at[j], small_recv.at[j], partner).start()
 
@@ -203,6 +203,18 @@
         to = dev(ctx + (2 if way else -2), tp)
         return remote(block, block, line_send.at[way, h, idx], line_recv.at[h, idx], to)
 
+    def piece(way, t):
+        s, h = lax.div(t + heads, heads) - 1, lax.rem(t + heads, heads)
+        idx = w - s if way else w + s
+        return h, idx, (s >= 0) & (idx >= 0) & (idx < W) & goes(way, h)
+
+    def pace(way, t):
+        h, idx, there = piece(way, t - 2)
+
+        @pl.when(there)
+        def _():
+            line_copy(h, idx, way).wait_send()
+
     def sib_copy(h, idx):
         block = kv_buf.at[h, idx, c]
         return remote(block, block, sib_send.at[h, idx], sib_recv.at[h, idx], sibling)
@@ -220,8 +232,9 @@
         same = lax.broadcasted_iota(jnp.int32, square, 0) == lax.broadcasted_iota(jnp.int32, square, 1)
         return jnp.sum(jnp.where(same, jnp.broadcast_to(line, square), 0), -1, keepdims=True)
 
-    def attend(h, blocks):
-        def one(k, _):
+    def attend(h, blocks, last):
+        def one(turn, _):
+            k = slots(h) - 1 - turn
             e = h + k * (heads - h)
             allowed = [
                 jnp.concatenate([pos_all[2 * idx], pos_all[2 * idx + 1]], axis=1) <= q_pos[k] for idx in blocks
@@ -251,6 +264,11 @@
                 fresh.append((now, sums, held))
             for a in range(2):
                 high[e, a], total[e, a], acc[e, a] = fresh[a]
+
+            @pl.when(last)
+            def _():
+                finish(h, k)
+
             return 0
 
         lax.fori_loop(0, slots(h), one, 0)
@@ -263,27 +281,22 @@
         to = dev(2 * (w + k * (mate - w)) + c, 2 * x + y)
         return remote(stage.at[e], normed.at[:, head_columns(h)], o_send.at[e], o_recv.at[h], to)
 
-    def finish(h):
-        def one(k, _):
-            e = h + k * (heads - h)
-            first = acc[e, 0] / total[e, 0, :, :1]
-            second = acc[e, 1] / total[e, 1, :, :1]
-            diff = first - lam_wide[h] * second
-            mean_square = jnp.mean(diff * diff, -1, keepdims=True)
-            result = (out_factor * diff * lax.rsqrt(mean_square + norm_eps) * gain_wide[h]).astype(jnp.bfloat16)
-
-            @pl.when(straight & (k == 0))
-            def _():
-                normed[:, head_columns(h)] = result
-
-            @pl.when(crossed | (k > 0))
-            def _():
-                stage[e] = result
-                o_copy(h, k).start()
-
-            return 0
-
-        lax.fori_loop(0, slots(h), one, 0)
+    def finish(h, k):
+        e = h + k * (heads - h)
+        first = acc[e, 0] / total[e, 0, :, :1]
+        second = acc[e, 1] / total[e, 1, :, :1]
+        diff = first - lam_wide[h] * second
+        mean_square = jnp.mean(diff * diff, -1, keepdims=True)
+        result = (out_factor * diff * lax.rsqrt(mean_square + norm_eps) * gain_wide[h]).astype(jnp.bfloat16)
+
+        @pl.when(straight & (k == 0))
+        def _():
+            normed[:, head_columns(h)] = result
+
+        @pl.when(crossed | (k > 0))
+        def _():
+            stage[e] = result
+            o_copy(h, k).start()
 
     res_copy.start()
 
@@ -296,6 +309,17 @@
 
         @pl.when(s == 0)
         def _():
+            for way in range(2):
+
+                @pl.when(straight & goes(way, h))
+                def _():
+                    pace(way, t)
+                    to = dev(ctx + (2 if way else -2), tp)
+                    own = pl.ds(pl.multiple_of(h * wide, wide), wide)
+                    for j, src in enumerate((k_in, v_in)):
+                        dst = kv_buf.at[h, w, y, :, pl.ds(j * wide, wide)]
+                        remote(src.at[:, own], dst, line_send.at[way, h, w], line_recv.at[h, w], to).start()
+
             cols = pl.ds(0, wide)
             src = k_in.at[:, cols]
             pltpu.make_async_copy(src, kv_buf.at[h, w, c, :, cols], init_recv.at[h, 0]).wait()
@@ -305,6 +329,7 @@
 
                 @pl.when(crossed & goes(way, h))
                 def _():
+                    pace(way, t)
                     line_copy(h, w, way).start()
 
             @pl.when(jnp.logical_not(left_out(h)))
@@ -312,6 +337,11 @@
                 sib_copy(h, w).start()
 
             pltpu.make_async_copy(src, q_buf.at[h], init_recv.at[h, 2]).wait()
+            for later in range(2, heads):
+
+                @pl.when(h == later - 2)
+                def _():
+                    init_start(later)
 
             @pl.when(left_out(h))
             def _():
@@ -338,12 +368,14 @@
                 @pl.when((idx >= 0) & (idx < W))
                 def _():
                     line_copy(h, idx, way).wait_recv()
-
-                    @pl.when(goes(way, h))
-                    def _():
-                        line_copy(h, idx, way).start()
-
                     sib_copy(h, idx).start()
+
+            for way, idx in ((1, w - s), (0, w + s)):
+
+                @pl.when((idx >= 0) & (idx < W) & goes(way, h))
+                def _():
+                    pace(way, t)
+                    line_copy(h, idx, way).start()
 
         lax.fori_loop(
             jnp.clip((t - 1) * w_per_step, 0, w_total), jnp.clip(t * w_per_step, 0, w_total), w_start, 0
@@ -369,23 +401,20 @@
             def _():
                 q_copy().wait_recv()
 
+            last = s1 == jnp.maximum(w, W - 1 - w)
             on_left, on_right = w - s1 >= 0, (s1 > 0) & (w + s1 < W)
 
             @pl.when(on_left & on_right)
             def _():
                 sib_wait(h1, w - s1)
                 sib_wait(h1, w + s1)
-                attend(h1, (w - s1, w + s1))
+                attend(h1, (w - s1, w + s1), last)
 
             @pl.when(on_left != on_right)
             def _():
                 idx = jnp.where(on_left, w - s1, w + s1)
                 sib_wait(h1, idx)
-                attend(h1, (idx,))
-
-            @pl.when(s1 == jnp.maximum(w, W - 1 - w))
-            def _():
-                finish(h1)
+                attend(h1, (idx,), last)
 
         return 0
 
@@ -475,17 +504,21 @@
             def _():
                 sib_copy(h, idx).wait_send()
 
-            @pl.when((idx <= w) & goes(1, h) & (jnp.logical_not(left_out(h)) | (idx == w)))
-            def _():
-                line_copy(h, idx, 1).wait_send()
-
-            @pl.when((idx >= w) & goes(0, h) & (jnp.logical_not(left_out(h)) | (idx == w)))
-            def _():
-                line_copy(h, idx, 0).wait_send()
-
         return 0
 
     lax.fori_loop(0, W, line_done, 0)
+
+    def piece_done(t, _):
+        for way in range(2):
+            h, idx, there = piece(way, t)
+
+            @pl.when(there & jnp.logical_not(piece(way, t + 2)[2]))
+            def _():
+                line_copy(h, idx, way).wait_send()
+
+        return 0
+
+    lax.fori_loop(0, W * heads, piece_done, 0)
 
     def last_chunk(j, _):
         cols = pl.ds(pl.multiple_of(j * CHUNK, CHUNK), CHUNK)

time: 53.6 us -> 53 us (0.989)
  Pallas kernels: 51.7 us -> 51 us
    pallas_call x1, Pallas kernels: 51.7 us -> 51 us  [per_device(): pl.pallas_call(functools.partial(layer_kernel, n_ctx, n_tp), out_shape=ja...]
where the time goes in v6:
time: 53 us; the launch traced here: 52.8 us
  Pallas kernels  51 us (96%)
  local copies, waits for them, and re-layouts  1.75 us (3%)
    pallas_call x1, Pallas kernels, per_device(): pl.pallas_call(functools.partial(layer_kernel, n_ctx, n_tp), out_shape=ja...  51 us
    unnamed x1, local copies, waits for them, and re-layouts  1.75 us

profile of v6, /device:TPU:0, one launch (start us, length us, event | category | flops | bytes accessed | tf_op | source)
XLA Modules:
  0.0 52.8 jit_solution(13098450820354641221)
XLA Ops:
  0.0 51.0 %attend_and_project.1 = bf16[144,1280]{1,0:T(8,128)(2,1)} custom-call(bf16[144,768]{1,0:T(8,128)(2,1)} %q_in.1, bf16[144,768]{1,0:T(8,128)(2,1)} %k_in.1, bf16[144,768]{1,0:T(8,128)(2,1)} %v_in.1, s32[1,144]{1,0:T(1,128)} %bitcast.5, f32[3,4,128]{2,1,0:T(4,128)} %bitcast.3, f32[6,128]{1,0:T(8,128)} %bitcast.4, bf16[768,5120]{1,0:T(8,128)(2,1)} %w_in.1, ...), custom_call_target="tpu_custom_call" | custom-call | tf_op jit(solution)/shard_map/attend_and_project/pallas_call | solution.py:548
  51.1 1.7 %copy.10 = bf16[144,1280]{1,0:T(8,128)(2,1)} copy(bf16[144,1280]{1,0:T(8,128)(2,1)} %attend_and_project.1) | data formatting | bytes 737280

commit v7 on v6

--- a/solution.py
+++ b/solution.py
@@ -13,7 +13,11 @@
 norm_eps = 1e-05
 MASKED = -3e38
 LOWEST = -1e30
-CHUNK = 256
+
+
+def column_cuts(columns):
+    edges = [0] + list(range(256, columns, 512)) + [columns]
+    return list(zip(edges[:-1], edges[1:]))
 
 
 def layer_kernel(
@@ -43,6 +47,7 @@
     normed,
     w_buf,
     res_buf,
+    base,
     part_sib,
     got_sib,
     part,
@@ -73,7 +78,8 @@
     depth = wide // 2
     W = n_ctx // 2
     X = n_tp // 2
-    n_chunk = w_buf.shape[1]
+    columns = w_buf.shape[2]
+    cuts = column_cuts(columns)
     off = heads - 1 if W >= 4 else -1
     scale = math.log2(math.e) / math.sqrt(depth)
     ctx = lax.axis_index("ctx")
@@ -184,16 +190,13 @@
     pltpu.make_async_copy(pos_in, pos_all.at[ctx], pos_recv.at[ctx]).start()
     lax.fori_loop(1, n_ctx, pos_start, 0)
 
-    def w_copy(i, j):
-        start = pl.multiple_of((i * n_chunk + j) * CHUNK, CHUNK)
-        return pltpu.make_async_copy(w_in.at[:, pl.ds(start, CHUNK)], w_buf.at[i, j], w_sem.at[i, j])
-
-    w_total = n_tp * n_chunk
-    w_per_step = -(-w_total // (W * heads - 1))
+    def w_copy(i):
+        start = pl.multiple_of(i * columns, 128)
+        return pltpu.make_async_copy(w_in.at[:, pl.ds(start, columns)], w_buf.at[i], w_sem.at[i])
 
     def w_start(k, _):
-        i, core = lax.rem(lax.div(k, 2 * n_chunk) + x + 1, X), lax.rem(lax.div(k, n_chunk) + c + 1, 2)
-        w_copy(2 * i + core, lax.rem(k, n_chunk)).start()
+        i, core = lax.rem(lax.div(k, 2) + x + 1, X), lax.rem(k + c + 1, 2)
+        w_copy(2 * i + core).start()
         return 0
 
     res_copy = pltpu.make_async_copy(res_in, res_buf, res_sem)
@@ -377,9 +380,7 @@
                     pace(way, t)
                     line_copy(h, idx, way).start()
 
-        lax.fori_loop(
-            jnp.clip((t - 1) * w_per_step, 0, w_total), jnp.clip(t * w_per_step, 0, w_total), w_start, 0
-        )
+        lax.fori_loop(jnp.clip(t - 1, 0, n_tp), jnp.clip(t, 0, n_tp), w_start, 0)
 
         @pl.when(t == 1)
         def _():
@@ -426,49 +427,46 @@
         def _():
             o_copy(h, 0).wait_recv()
 
-    def product(i, core, j):
+    def product(i, core, lo, hi):
         target = 2 * lax.rem(x + i, X) + core
-        w_copy(target, j).wait()
-        return jnp.dot(normed[...], w_buf[target, j], preferred_element_type=jnp.float32)
-
-    def ps_copy(i, j):
-        return remote(part_sib.at[i, j], got_sib.at[i, j], ps_send.at[i, j], ps_recv.at[i, j], sibling)
+        return jnp.dot(normed[...], w_buf[target, :, lo:hi], preferred_element_type=jnp.float32)
+
+    def w_wait(i, core):
+        w_copy(2 * lax.rem(x + i, X) + core).wait()
+
+    def ps_copy(i, j, lo, hi):
+        cols = pl.ds(lo, hi - lo)
+        return remote(part_sib.at[i, :, cols], got_sib.at[i, :, cols], ps_send.at[i, j], ps_recv.at[i, j], sibling)
 
     def p_copy(i, j):
+        lo, hi = cuts[j]
+        cols = pl.ds(lo, hi - lo)
         to = dev(ctx, 2 * lax.rem(x + i, X) + c)
-        return remote(part.at[i - 1, j], got.at[i - 1, j], p_send.at[i - 1, j], p_recv.at[i - 1, j], to)
-
-    def give_sibling(i):
-        def body(j, _):
-            part_sib[i, j] = product(i, 1 - c, j).astype(jnp.bfloat16)
-            ps_copy(i, j).start()
-            return 0
-
-        lax.fori_loop(0, n_chunk, body, 0)
-
-    def pair_sum(i, j):
-        mine = product(i, c, j)
-        ps_copy(i, j).wait_recv()
-        return mine + got_sib[i, j].astype(jnp.float32)
+        return remote(
+            part.at[i - 1, :, cols], got.at[i - 1, :, cols], p_send.at[i - 1, j], p_recv.at[i - 1, j], to
+        )
+
+    def give_sibling(i, j, lo, hi):
+        part_sib[i, :, lo:hi] = product(i, 1 - c, lo, hi).astype(jnp.bfloat16)
+        ps_copy(i, j, lo, hi).start()
 
     for i in range(1, X):
-
-        def send_chunk(j, _):
-            @pl.when(j < n_chunk)
-            def _():
-                part_sib[i, j] = product(i, 1 - c, j).astype(jnp.bfloat16)
-                ps_copy(i, j).start()
-
-            @pl.when(j >= 2)
-            def _():
-                part[i - 1, j - 2] = pair_sum(i, j - 2).astype(jnp.bfloat16)
-                p_copy(i, j - 2).start()
-
-            return 0
-
-        lax.fori_loop(0, n_chunk + 2, send_chunk, 0)
-    give_sibling(0)
+        w_wait(i, 1 - c)
+        w_wait(i, c)
+        for j in range(len(cuts) + 1):
+            if j < len(cuts):
+                give_sibling(i, j, *cuts[j])
+            if j >= 1:
+                lo, hi = cuts[j - 1]
+                mine = product(i, c, lo, hi)
+                ps_copy(i, j - 1, lo, hi).wait_recv()
+                part[i - 1, :, lo:hi] = (mine + got_sib[i, :, lo:hi].astype(jnp.float32)).astype(jnp.bfloat16)
+                p_copy(i, j - 1).start()
+    w_wait(0, 1 - c)
+    w_wait(0, c)
+    give_sibling(0, 0, 0, columns)
     res_copy.wait()
+    base[...] = product(0, c, 0, columns) + res_buf[...].astype(jnp.float32)
 
     def pos_done(i, _):
         pos_copy(i).wait_send()
@@ -520,18 +518,16 @@
 
     lax.fori_loop(0, W * heads, piece_done, 0)
 
-    def last_chunk(j, _):
-        cols = pl.ds(pl.multiple_of(j * CHUNK, CHUNK), CHUNK)
-        result = pair_sum(0, j) + res_buf[:, cols].astype(jnp.float32)
+    ps_copy(0, 0, 0, columns).wait()
+    for i in range(1, X):
+        for j, (lo, hi) in enumerate(cuts):
+            ps_copy(i, j, lo, hi).wait_send()
+    for j, (lo, hi) in enumerate(cuts):
+        result = base[:, lo:hi] + got_sib[0, :, lo:hi].astype(jnp.float32)
         for i in range(1, X):
             p_copy(i, j).wait()
-            result = result + got[i - 1, j].astype(jnp.float32)
-        for i in range(X):
-            ps_copy(i, j).wait_send()
-        out_ref[:, cols] = result.astype(out_ref.dtype)
-        return 0
-
-    lax.fori_loop(0, n_chunk, last_chunk, 0)
+            result = result + got[i - 1, :, lo:hi].astype(jnp.float32)
+        out_ref[:, lo:hi] = result.astype(out_ref.dtype)
 
 
 def per_device(n_ctx, n_tp, queries, keys, values, positions, lambda_vecs, head_gain, out_weight, residual):
@@ -540,7 +536,7 @@
     wide = 2 * depth
     W, X = n_ctx // 2, n_tp // 2
     columns = out_weight.shape[1] // n_tp
-    n_chunk = columns // CHUNK
+    n_cut = len(column_cuts(columns))
     vmem = pl.BlockSpec(memory_space=pltpu.VMEM)
     hbm = pl.BlockSpec(memory_space=pl.ANY)
     bf16, f32 = jnp.bfloat16, jnp.float32
@@ -564,12 +560,13 @@
             pltpu.VMEM((heads + 1, 2, rows, wide), f32),
             pltpu.VMEM((heads + 1, rows, wide), bf16),
             pltpu.VMEM((rows, heads * wide), bf16),
-            pltpu.VMEM((n_tp, n_chunk, heads * wide, CHUNK), bf16),
+            pltpu.VMEM((n_tp, heads * wide, columns), bf16),
             pltpu.VMEM((rows, columns), bf16),
-            pltpu.VMEM((X, n_chunk, rows, CHUNK), bf16),
-            pltpu.VMEM((X, n_chunk, rows, CHUNK), bf16),
-            pltpu.VMEM((X - 1, n_chunk, rows, CHUNK), bf16),
-            pltpu.VMEM((X - 1, n_chunk, rows, CHUNK), bf16),
+            pltpu.VMEM((rows, columns), f32),
+            pltpu.VMEM((X, rows, columns), bf16),
+            pltpu.VMEM((X, rows, columns), bf16),
+            pltpu.VMEM((X - 1, rows, columns), bf16),
+            pltpu.VMEM((X - 1, rows, columns), bf16),
             dma((heads, 3)),
             dma((heads, 3)),
             dma((2,)),
@@ -584,12 +581,12 @@
             dma(()),
             dma((heads + 1,)),
             dma((heads,)),
-            dma((n_tp, n_chunk)),
+            dma((n_tp,)),
             dma(()),
-            dma((X, n_chunk)),
-            dma((X, n_chunk)),
-            dma((X - 1, n_chunk)),
-            dma((X - 1, n_chunk)),
+            dma((X, n_cut)),
+            dma((X, n_cut)),
+            dma((X - 1, n_cut)),
+            dma((X - 1, n_cut)),
         ],
         compiler_params=pltpu.CompilerParams(
             collective_id=0, has_side_effects=True, vmem_limit_bytes=56 * 1024 * 1024

time: 53 us -> 52.6 us (level)
  no operation moved by 1% of the time
where the time goes in v7:
time: 52.6 us; the launch traced here: 52.4 us
  Pallas kernels  50.7 us (96%)
  local copies, waits for them, and re-layouts  1.75 us (3%)
    pallas_call x1, Pallas kernels, per_device(): pl.pallas_call(functools.partial(layer_kernel, n_ctx, n_tp), out_shape=ja...  50.7 us
    unnamed x1, local copies, waits for them, and re-layouts  1.75 us

profile of v7, /device:TPU:0, one launch (start us, length us, event | category | flops | bytes accessed | tf_op | source)
XLA Modules:
  0.0 52.4 jit_solution(17458989561910779584)
XLA Ops:
  0.0 50.7 %attend_and_project.1 = bf16[144,1280]{1,0:T(8,128)(2,1)} custom-call(bf16[144,768]{1,0:T(8,128)(2,1)} %q_in.1, bf16[144,768]{1,0:T(8,128)(2,1)} %k_in.1, bf16[144,768]{1,0:T(8,128)(2,1)} %v_in.1, s32[1,144]{1,0:T(1,128)} %bitcast.5, f32[3,4,128]{2,1,0:T(4,128)} %bitcast.3, f32[6,128]{1,0:T(8,128)} %bitcast.4, bf16[768,5120]{1,0:T(8,128)(2,1)} %w_in.1, ...), custom_call_target="tpu_custom_call" | custom-call | tf_op jit(solution)/shard_map/attend_and_project/pallas_call | solution.py:544
  50.7 1.7 %copy.10 = bf16[144,1280]{1,0:T(8,128)(2,1)} copy(bf16[144,1280]{1,0:T(8,128)(2,1)} %attend_and_project.1) | data formatting | bytes 737280

commit v8 on v7

--- a/solution.py
+++ b/solution.py
@@ -115,31 +115,6 @@
     sibling = dev(ctx, 2 * x + 1 - c)
     far = dev(2 * mate + c, 2 * x + y)
 
-    barrier = pltpu.get_barrier_semaphore()
-
-    def greet(to):
-        pl.semaphore_signal(barrier, inc=1, device_id=to, device_id_type=pl.DeviceIdType.MESH)
-
-    greet(sibling)
-
-    @pl.when(crossed)
-    def _():
-        greet(partner)
-
-    @pl.when(crossed & (at_end | helper))
-    def _():
-        greet(far)
-
-    for i in range(1, X):
-        greet(dev(ctx, 2 * lax.rem(x + i, X) + c))
-
-    def greet_row(i, _):
-        greet(dev(lax.rem(ctx + i, n_ctx), tp))
-        return 0
-
-    lax.fori_loop(1, n_ctx, greet_row, 0)
-    pl.semaphore_wait(barrier, n_ctx - 1 + 1 + X - 1 + lax.rem(c + y, 2) + jnp.where(crossed & (at_end | helper), 1, 0))
-
     def init_pairs(h):
         cols = pl.ds(h * wide, wide)
         return (
@@ -150,12 +125,51 @@
 
     small_pairs = ((lam_in, lam_buf), (gain_in, gain_buf))
 
-    def init_start(h):
-        @pl.when(straight)
-        def _():
+    def w_copy(i):
+        start = pl.multiple_of(i * columns, 128)
+        return pltpu.make_async_copy(w_in.at[:, pl.ds(start, columns)], w_buf.at[i], w_sem.at[i])
+
+    res_copy = pltpu.make_async_copy(res_in, res_buf, res_sem)
+
+    @pl.when(straight)
+    def _():
+        for h in range(heads):
             for j, (src, dst) in enumerate(init_pairs(h)):
                 pltpu.make_async_copy(src, dst, init_recv.at[h, j]).start()
-
+        for j, (src, dst) in enumerate(small_pairs):
+            pltpu.make_async_copy(src, dst, small_recv.at[j]).start()
+
+    pltpu.make_async_copy(pos_in, pos_all.at[ctx], pos_recv.at[ctx]).start()
+    for k in range(2 * X):
+        w_copy(2 * lax.rem(x + k // 2 + 1, X) + lax.rem(c + k + 1, 2)).start()
+    res_copy.start()
+
+    barrier = pltpu.get_barrier_semaphore()
+
+    def greet(to):
+        pl.semaphore_signal(barrier, inc=1, device_id=to, device_id_type=pl.DeviceIdType.MESH)
+
+    greet(sibling)
+
+    @pl.when(crossed)
+    def _():
+        greet(partner)
+
+    @pl.when(crossed & (at_end | helper))
+    def _():
+        greet(far)
+
+    for i in range(1, X):
+        greet(dev(ctx, 2 * lax.rem(x + i, X) + c))
+
+    def greet_row(i, _):
+        greet(dev(lax.rem(ctx + i, n_ctx), tp))
+        return 0
+
+    lax.fori_loop(1, n_ctx, greet_row, 0)
+    pl.semaphore_wait(barrier, n_ctx - 1 + 1 + X - 1 + lax.rem(c + y, 2) + jnp.where(crossed & (at_end | helper), 1, 0))
+
+    def init_start(h):
         @pl.when(crossed)
         def _():
             for j, (src, dst) in enumerate(init_pairs(h)):
@@ -163,11 +177,6 @@
 
     for h in range(min(2, heads)):
         init_start(h)
-
-    @pl.when(straight)
-    def _():
-        for j, (src, dst) in enumerate(small_pairs):
-            pltpu.make_async_copy(src, dst, small_recv.at[j]).start()
 
     @pl.when(crossed)
     def _():
@@ -187,19 +196,7 @@
         pos_copy(i).start()
         return 0
 
-    pltpu.make_async_copy(pos_in, pos_all.at[ctx], pos_recv.at[ctx]).start()
     lax.fori_loop(1, n_ctx, pos_start, 0)
-
-    def w_copy(i):
-        start = pl.multiple_of(i * columns, 128)
-        return pltpu.make_async_copy(w_in.at[:, pl.ds(start, columns)], w_buf.at[i], w_sem.at[i])
-
-    def w_start(k, _):
-        i, core = lax.rem(lax.div(k, 2) + x + 1, X), lax.rem(k + c + 1, 2)
-        w_copy(2 * i + core).start()
-        return 0
-
-    res_copy = pltpu.make_async_copy(res_in, res_buf, res_sem)
 
     def line_copy(h, idx, way):
         block = kv_buf.at[h, idx, c]
@@ -301,8 +298,6 @@
             stage[e] = result
             o_copy(h, k).start()
 
-    res_copy.start()
-
     high[...] = jnp.full(high.shape, LOWEST, jnp.float32)
     total[...] = jnp.zeros(total.shape, jnp.float32)
     acc[...] = jnp.zeros(acc.shape, jnp.float32)
@@ -379,8 +374,6 @@
                 def _():
                     pace(way, t)
                     line_copy(h, idx, way).start()
-
-        lax.fori_loop(jnp.clip(t - 1, 0, n_tp), jnp.clip(t, 0, n_tp), w_start, 0)
 
         @pl.when(t == 1)
         def _():

time: 52.6 us -> 52.6 us (level)
  no operation moved by 1% of the time
where the time goes in v8:
time: 52.6 us; the launch traced here: 52.5 us
  Pallas kernels  50.7 us (96%)
  local copies, waits for them, and re-layouts  1.75 us (3%)
    pallas_call x1, Pallas kernels, per_device(): pl.pallas_call(functools.partial(layer_kernel, n_ctx, n_tp), out_shape=ja...  50.7 us
    unnamed x1, local copies, waits for them, and re-layouts  1.75 us

profile of v8, /device:TPU:0, one launch (start us, length us, event | category | flops | bytes accessed | tf_op | source)
XLA Modules:
  0.0 52.5 jit_solution(10856444686410267952)
XLA Ops:
  0.0 50.7 %attend_and_project.1 = bf16[144,1280]{1,0:T(8,128)(2,1)} custom-call(bf16[144,768]{1,0:T(8,128)(2,1)} %q_in.1, bf16[144,768]{1,0:T(8,128)(2,1)} %k_in.1, bf16[144,768]{1,0:T(8,128)(2,1)} %v_in.1, s32[1,144]{1,0:T(1,128)} %bitcast.5, f32[3,4,128]{2,1,0:T(4,128)} %bitcast.3, f32[6,128]{1,0:T(8,128)} %bitcast.4, bf16[768,5120]{1,0:T(8,128)(2,1)} %w_in.1, ...), custom_call_target="tpu_custom_call" | custom-call | tf_op jit(solution)/shard_map/attend_and_project/pallas_call | solution.py:537
  50.7 1.7 %copy.10 = bf16[144,1280]{1,0:T(8,128)(2,1)} copy(bf16[144,1280]{1,0:T(8,128)(2,1)} %attend_and_project.1) | data formatting | bytes 737280

commit v9 on v8

--- a/solution.py
+++ b/solution.py
@@ -209,7 +209,7 @@
         return h, idx, (s >= 0) & (idx >= 0) & (idx < W) & goes(way, h)
 
     def pace(way, t):
-        h, idx, there = piece(way, t - 2)
+        h, idx, there = piece(way, t - 3)
 
         @pl.when(there)
         def _():
@@ -503,7 +503,7 @@
         for way in range(2):
             h, idx, there = piece(way, t)
 
-            @pl.when(there & jnp.logical_not(piece(way, t + 2)[2]))
+            @pl.when(there & jnp.logical_not(piece(way, t + 3)[2]))
             def _():
                 line_copy(h, idx, way).wait_send()
 

time: 52.6 us -> 52.6 us (level)
  no operation moved by 1% of the time
where the time goes in v9:
time: 52.6 us; the launch traced here: 52.5 us
  Pallas kernels  50.7 us (96%)
  local copies, waits for them, and re-layouts  1.75 us (3%)
    pallas_call x1, Pallas kernels, per_device(): pl.pallas_call(functools.partial(layer_kernel, n_ctx, n_tp), out_shape=ja...  50.7 us
    unnamed x1, local copies, waits for them, and re-layouts  1.75 us

profile of v9, /device:TPU:0, one launch (start us, length us, event | category | flops | bytes accessed | tf_op | source)
XLA Modules:
  0.0 52.5 jit_solution(17345015506826923620)
XLA Ops:
  0.0 50.7 %attend_and_project.1 = bf16[144,1280]{1,0:T(8,128)(2,1)} custom-call(bf16[144,768]{1,0:T(8,128)(2,1)} %q_in.1, bf16[144,768]{1,0:T(8,128)(2,1)} %k_in.1, bf16[144,768]{1,0:T(8,128)(2,1)} %v_in.1, s32[1,144]{1,0:T(1,128)} %bitcast.5, f32[3,4,128]{2,1,0:T(4,128)} %bitcast.3, f32[6,128]{1,0:T(8,128)} %bitcast.4, bf16[768,5120]{1,0:T(8,128)(2,1)} %w_in.1, ...), custom_call_target="tpu_custom_call" | custom-call | tf_op jit(solution)/shard_map/attend_and_project/pallas_call | solution.py:537
  50.7 1.7 %copy.10 = bf16[144,1280]{1,0:T(8,128)(2,1)} copy(bf16[144,1280]{1,0:T(8,128)(2,1)} %attend_and_project.1) | data formatting | bytes 737280
